TPU v7x, 512 devices: a whole 4x4x16 slice. The times are simulated.
512 devices in a mesh: dir: 4 (over x), tex: 128 (over z, y, core).
Axes of the slice: x: 4, y: 4, z: 16, core: 2. Of those that a mesh axis runs over, the one named last changes fastest.
Arguments:
- slab: bfloat16 [131072, 4096], P('tex', 'dir'), may hold values from -4 to 4
- exponents: int32 [1024, 32], P('tex', 'dir'), may hold values from -2 to 2
- sketch: bfloat16 [4096, 512], P('dir'), may hold values from -0.09375 to 0.09375
Outputs:
- basis: bfloat16 [131072, 512], P(('tex', 'dir'))
All inputs are finite; a program needn't handle non-finite values.
Results may differ from a plain program's by a relative error of at most 0.02.
Values may be sent and summed in bfloat16 or wider, within the bound.
No kernel may reach another device: no remote copies, remote signals or barrier semaphores. Data moves between devices by JAX's collectives and lax.ppermute only.
A program may use at most 64 MiB of HBM per device.

v0:
```python
import math

import jax
import jax.numpy as jnp
from jax import lax
from jax.sharding import PartitionSpec as P


def from_partner(block, axis, bit):
    count = lax.axis_size(axis)
    route = []
    for low in range(count):
        high = low | 1 << bit
        if high != low and high < count:
            route += [(low, high), (high, low)]
    return lax.ppermute(block, axis, route)


def scales_of(exponent_table):
    total = jnp.zeros(exponent_table.shape, jnp.float32)
    for exponent_value in range(-2, 3):
        total = total + jnp.where(
            exponent_table == exponent_value, jnp.float32(2.0**exponent_value), jnp.float32(0.0)
        )
    return total.astype(jnp.bfloat16)


def dequantize(values, exponent_table):
    height, breadth = values.shape
    edge_rows = height // exponent_table.shape[0]
    edge_cols = breadth // exponent_table.shape[1]
    scale_table = scales_of(exponent_table)
    tiled = values.reshape(exponent_table.shape[0], edge_rows, exponent_table.shape[1], edge_cols)
    tiled = tiled * scale_table[:, None, :, None]
    return tiled.reshape(height, breadth)


def column_gram(matrix):
    return lax.dot_general(
        matrix, matrix, (((0,), (0,)), ((), ())), precision=lax.Precision.HIGHEST
    )


def right_solve(lower_factor, matrix):
    return lax.linalg.triangular_solve(
        lower_factor, matrix, left_side=False, lower=True, transpose_a=True
    )


def body(slab, exponents, sketch):
    scaled_values = dequantize(slab, exponents)
    sketched = lax.psum_scatter(
        jnp.dot(scaled_values, sketch, preferred_element_type=jnp.float32).astype(jnp.bfloat16),
        "dir",
        scatter_dimension=0,
        tiled=True,
    ).astype(jnp.float32)
    merged_gram = lax.psum(column_gram(sketched).astype(jnp.bfloat16), "dir").astype(jnp.float32)
    levels = lax.axis_size("tex").bit_length() - 1
    for level_bit in range(levels):
        partner = from_partner(merged_gram.astype(jnp.bfloat16), "tex", level_bit).astype(
            merged_gram.dtype
        )
        merged_gram = merged_gram + partner
    lower_factor = jnp.linalg.cholesky(merged_gram)
    orthonormal = right_solve(lower_factor, sketched)
    texel_count = sketched.shape[0] * lax.axis_size(("dir", "tex"))
    return (orthonormal * math.sqrt(texel_count)).astype(jnp.bfloat16)


def solution(mesh):
    return jax.shard_map(
        body,
        mesh=mesh,
        in_specs=(P("tex", "dir"), P("tex", "dir"), P("dir", None)),
        out_specs=P(("tex", "dir"), None),
        check_vma=False,
    )
```

profile of v0, /device:TPU:1, one launch (start us, length us, event | category | flops | bytes accessed | tf_op | source)
XLA Modules:
  0.0 437.1 jit_solution(96111827553857974)
XLA Ops:
  6.5 0.8 add_convert_fusion
  7.8 0.7 copy-done.6
  8.5 2.2 fusion.2
  10.8 34.5 %reduce-scatter.2.cloned.1.call-done = bf16[256,512]{1,0:T(8,128)(2,1)} async-done(((bf16[1024,512]{1,0:T(8,128)(2,1)}), bf16[256,512]{1,0:T(8,128)(2,1)}) %reduce-scatter.2.cloned.1.call-update) | async-done | bytes 262160 | tf_op jit(solution)/shard_map/reduce_scatter | solution.py:52
  45.3 2.2 convolution_convert_fusion
  47.5 58.5 %all-reduce.3.cloned.1.call-done = bf16[512,512]{0,1:T(8,128)(2,1)} async-done(((bf16[512,512]{0,1:T(8,128)(2,1)}), bf16[512,512]{0,1:T(8,128)(2,1)}) %all-reduce.3.cloned.1.call-update) | async-done | bytes 524304 | tf_op jit(solution)/shard_map/psum | solution.py:58
  106.0 4.8 %collective-permute-start = (bf16[512,512]{0,1:T(8,128)(2,1)}, bf16[512,512]{0,1:T(8,128)(2,1)S(1)}, u32[]{:S(2)}, u32[]{:S(2)}) collective-permute-start(bf16[512,512]{0,1:T(8,128)(2,1)} %all-reduce.3.cloned.1.call-done), channel_id=1, source_target_pairs={{0,1},{1,0},{2,3},{3,2},{4,5},{5,4},{6,7},{7,6},{8,9},{9,8},{10,11... | collective-permute-start | bytes 1572872 | tf_op jit(solution)/shard_map/ppermute | solution.py:16
  110.8 1.7 collective-permute-done
  112.5 1.2 fusion.4
  113.7 3.1 collective-permute-start.1
  116.8 11.9 %collective-permute-done.1 = bf16[512,512]{0,1:T(8,128)(2,1)S(1)} collective-permute-done((bf16[512,512]{0,1:T(8,128)(2,1)S(1)}, bf16[512,512]{0,1:T(8,128)(2,1)S(1)}, u32[]{:S(2)}, u32[]{:S(2)}) %collective-permute-start.1) | collective-permute-done | bytes 524320 | tf_op jit(solution)/shard_map/ppermute | solution.py:16
  128.7 1.2 fusion.14
  130.0 4.6 %collective-permute-start.2 = (bf16[512,512]{0,1:T(8,128)(2,1)S(1)}, bf16[512,512]{0,1:T(8,128)(2,1)S(1)}, u32[]{:S(2)}, u32[]{:S(2)}) collective-permute-start(bf16[512,512]{0,1:T(8,128)(2,1)S(1)} %fusion.14), channel_id=1, source_target_pairs={{0,4},{4,0},{1,5},{5,1},{2,6},{6,2},{3,7},{7,3},{8,12},{12,8},{9,1... | collective-permute-start | bytes 1572872 | tf_op jit(solution)/shard_map/ppermute | solution.py:16
  134.6 11.0 %collective-permute-done.2 = bf16[512,512]{0,1:T(8,128)(2,1)S(1)} collective-permute-done((bf16[512,512]{0,1:T(8,128)(2,1)S(1)}, bf16[512,512]{0,1:T(8,128)(2,1)S(1)}, u32[]{:S(2)}, u32[]{:S(2)}) %collective-permute-start.2) | collective-permute-done | bytes 524320 | tf_op jit(solution)/shard_map/ppermute | solution.py:16
  145.9 3.2 collective-permute-start.3
  149.1 10.0 %collective-permute-done.3 = bf16[512,512]{0,1:T(8,128)(2,1)S(1)} collective-permute-done((bf16[512,512]{0,1:T(8,128)(2,1)S(1)}, bf16[512,512]{0,1:T(8,128)(2,1)S(1)}, u32[]{:S(2)}, u32[]{:S(2)}) %collective-permute-start.3) | collective-permute-done | bytes 524320 | tf_op jit(solution)/shard_map/ppermute | solution.py:16
  159.5 4.2 collective-permute-start.4
  163.7 22.6 %collective-permute-done.4 = bf16[512,512]{0,1:T(8,128)(2,1)S(1)} collective-permute-done((bf16[512,512]{0,1:T(8,128)(2,1)S(1)}, bf16[512,512]{0,1:T(8,128)(2,1)S(1)}, u32[]{:S(2)}, u32[]{:S(2)}) %collective-permute-start.4) | collective-permute-done | bytes 524320 | tf_op jit(solution)/shard_map/ppermute | solution.py:16
  186.5 7.5 %collective-permute-start.5 = (bf16[512,512]{0,1:T(8,128)(2,1)S(1)}, bf16[512,512]{0,1:T(8,128)(2,1)S(1)}, u32[]{:S(2)}, u32[]{:S(2)}) collective-permute-start(bf16[512,512]{0,1:T(8,128)(2,1)S(1)} %fusion.6), channel_id=1, source_target_pairs={{0,32},{32,0},{1,33},{33,1},{2,34},{34,2},{3,35},{35,3},{4,36},{36... | collective-permute-start | bytes 1572872 | tf_op jit(solution)/shard_map/ppermute | solution.py:16
  194.0 56.4 %collective-permute-done.5 = bf16[512,512]{0,1:T(8,128)(2,1)S(1)} collective-permute-done((bf16[512,512]{0,1:T(8,128)(2,1)S(1)}, bf16[512,512]{0,1:T(8,128)(2,1)S(1)}, u32[]{:S(2)}, u32[]{:S(2)}) %collective-permute-start.5) | collective-permute-done | bytes 524320 | tf_op jit(solution)/shard_map/ppermute | solution.py:16
  250.6 11.3 %collective-permute-start.6 = (bf16[512,512]{0,1:T(8,128)(2,1)S(1)}, bf16[512,512]{0,1:T(8,128)(2,1)}, u32[]{:S(2)}, u32[]{:S(2)}) collective-permute-start(bf16[512,512]{0,1:T(8,128)(2,1)S(1)} %fusion.8), channel_id=1, source_target_pairs={{0,64},{64,0},{1,65},{65,1},{2,66},{66,2},{3,67},{67,3},{4,68},{68... | collective-permute-start | bytes 1572872 | tf_op jit(solution)/shard_map/ppermute | solution.py:16
  262.0 0.9 convert_element_type.75
  262.9 19.7 %collective-permute-done.6 = bf16[512,512]{0,1:T(8,128)(2,1)} collective-permute-done((bf16[512,512]{0,1:T(8,128)(2,1)S(1)}, bf16[512,512]{0,1:T(8,128)(2,1)}, u32[]{:S(2)}, u32[]{:S(2)}) %collective-permute-start.6) | collective-permute-done | bytes 524320 | tf_op jit(solution)/shard_map/ppermute | solution.py:16
  282.6 1.6 convert_add_fusion
  284.8 1.0 copy-done.3
  285.8 11.7 %cholesky.104 = f32[128,128]{1,0:T(8,128)S(1)} custom-call(f32[128,128]{1,0:T(8,128)S(1)} %cholesky.266), custom_call_target="Cholesky" | custom-call | tf_op jit(solution)/shard_map/jit(cholesky)/cholesky | solution.py:65
  297.7 9.8 %custom-call.30 = f32[1,128,128]{1,2,0:T(8,128)S(1)} custom-call(f32[1,128,128]{2,1,0:T(8,128)S(1)} %get-tuple-element.34), custom_call_target="InvertDiagBlocksLowerTriangular" | custom-call | tf_op jit(solution)/shard_map/jit(cholesky)/cholesky | solution.py:65
  307.5 1.2 constant_dynamic-update-slice_fusion.3
  308.8 1.3 convolution_subtract_fusion
  310.0 11.7 %cholesky.217 = f32[128,128]{1,0:T(8,128)S(1)} custom-call(f32[128,128]{1,0:T(8,128)S(1)} %cholesky.270), custom_call_target="Cholesky" | custom-call | tf_op jit(solution)/shard_map/jit(cholesky)/cholesky | solution.py:65
  321.8 10.0 %custom-call.31 = f32[1,128,128]{1,2,0:T(8,128)S(1)} custom-call(f32[1,128,128]{2,1,0:T(8,128)S(1)} %get-tuple-element.31), custom_call_target="InvertDiagBlocksLowerTriangular" | custom-call | tf_op jit(solution)/shard_map/jit(cholesky)/cholesky | solution.py:65
  332.0 1.3 convolution_subtract_fusion.3
  333.3 11.7 %cholesky.238 = f32[128,128]{1,0:T(8,128)S(1)} custom-call(f32[128,128]{1,0:T(8,128)S(1)} %cholesky.275), custom_call_target="Cholesky" | custom-call | tf_op jit(solution)/shard_map/jit(cholesky)/cholesky | solution.py:65
  345.8 9.8 %custom-call.32 = f32[1,128,128]{1,2,0:T(8,128)S(1)} custom-call(f32[1,128,128]{2,1,0:T(8,128)S(1)} %get-tuple-element.28), custom_call_target="InvertDiagBlocksLowerTriangular" | custom-call | tf_op jit(solution)/shard_map/jit(cholesky)/cholesky | solution.py:65
  355.8 1.2 convolution_subtract_fusion.5
  357.0 11.9 %cholesky.255 = f32[128,128]{1,0:T(8,128)S(1)} custom-call(f32[128,128]{1,0:T(8,128)S(1)} %convolution_subtract_fusion.5), custom_call_target="Cholesky" | custom-call | tf_op jit(solution)/shard_map/jit(cholesky)/cholesky | solution.py:65
  368.9 0.7 compare_reduce_fusion
  369.6 0.7 compare_reduce_fusion.2
  373.0 10.5 %while.1 = (s32[]{:T(128)}, f32[512,512]{1,0:T(8,128)S(1)}, s32[4,2]{0,1:T(2,128)S(1)}, f32[4,128,128]{2,1,0:T(8,128)}, s32[]{:T(128)}) while((s32[]{:T(128)}, f32[512,512]{1,0:T(8,128)S(1)}, s32[4,2]{0,1:T(2,128)S(1)}, f32[4,128,128]{2,1,0:T(8,128)}, s32[]{:T(128)}) %tuple.28), condition=%wide.while_cond, body=%wide.while_body.sunk | while | flops 2 | bytes 132705 | solution.py:45
  373.7 2.0 bitcast_dynamic-update-slice_fusion.2
  376.3 2.0 bitcast_dynamic-update-slice_fusion.2
  378.9 2.0 bitcast_dynamic-update-slice_fusion.2
  381.5 2.0 bitcast_dynamic-update-slice_fusion.2
  383.5 40.1 %custom-call.33 = f32[4,128,128]{1,2,0:T(8,128)S(1)} custom-call(f32[4,128,128]{2,1,0:T(8,128)} %get-tuple-element.12), custom_call_target="InvertDiagBlocksLowerTriangular" | custom-call | tf_op jit(solution)/shard_map/triangular_solve | solution.py:45
  423.9 1.3 convolution_subtract_fusion.4
  425.5 1.5 convolution_subtract_fusion.2
  427.4 1.7 convolution_subtract_fusion.1
  429.5 0.8 copy.6
  (51 shorter events, 7.5 us)
Async XLA Ops:
  6.5 1.2 copy-start
  6.5 1.9 copy-start.6
  6.5 38.7 %reduce-scatter.2.cloned.1.call-start = ((), (), s32[]{:S(2)}) async-start(), calls=%async_computation.1 | async-start | bytes 1310720 | tf_op jit(solution)/shard_map/reduce_scatter | solution.py:52
  10.7 95.2 %all-reduce.3.cloned.1.call-start = ((), (), s32[]{:S(2)}) async-start(), calls=%async_computation.2 | async-start | bytes 1048576 | tf_op jit(solution)/shard_map/psum | solution.py:58
  106.0 39.7 %copy-start.1 = (bf16[512,512]{0,1:T(8,128)(2,1)S(1)}, bf16[512,512]{0,1:T(8,128)(2,1)}, u32[]{:S(2)}) copy-start(bf16[512,512]{0,1:T(8,128)(2,1)} %all-reduce.3.cloned.1.call-done) | copy-start | bytes 1572868
  106.0 6.6 %collective-permute-start = (bf16[512,512]{0,1:T(8,128)(2,1)}, bf16[512,512]{0,1:T(8,128)(2,1)S(1)}, u32[]{:S(2)}, u32[]{:S(2)}) collective-permute-start(bf16[512,512]{0,1:T(8,128)(2,1)} %all-reduce.3.cloned.1.call-done), channel_id=1, source_target_pairs={{0,1},{1,0},{2,3},{3,2},{4,5},{5,4},{6,7},{7,6},{8,9},{9,8},{10,11... | collective-permute-start | bytes 1572872 | tf_op jit(solution)/shard_map/ppermute | solution.py:16
  113.7 15.0 %collective-permute-start.1 = (bf16[512,512]{0,1:T(8,128)(2,1)S(1)}, bf16[512,512]{0,1:T(8,128)(2,1)S(1)}, u32[]{:S(2)}, u32[]{:S(2)}) collective-permute-start(bf16[512,512]{0,1:T(8,128)(2,1)S(1)} %fusion.4), channel_id=1, source_target_pairs={{0,2},{2,0},{1,3},{3,1},{4,6},{6,4},{5,7},{7,5},{8,10},{10,8},{9,1... | collective-permute-start | bytes 1572872 | tf_op jit(solution)/shard_map/ppermute | solution.py:16
  130.0 15.6 %collective-permute-start.2 = (bf16[512,512]{0,1:T(8,128)(2,1)S(1)}, bf16[512,512]{0,1:T(8,128)(2,1)S(1)}, u32[]{:S(2)}, u32[]{:S(2)}) collective-permute-start(bf16[512,512]{0,1:T(8,128)(2,1)S(1)} %fusion.14), channel_id=1, source_target_pairs={{0,4},{4,0},{1,5},{5,1},{2,6},{6,2},{3,7},{7,3},{8,12},{12,8},{9,1... | collective-permute-start | bytes 1572872 | tf_op jit(solution)/shard_map/ppermute | solution.py:16
  145.9 13.2 %collective-permute-start.3 = (bf16[512,512]{0,1:T(8,128)(2,1)S(1)}, bf16[512,512]{0,1:T(8,128)(2,1)S(1)}, u32[]{:S(2)}, u32[]{:S(2)}) collective-permute-start(bf16[512,512]{0,1:T(8,128)(2,1)S(1)} %fusion.5), channel_id=1, source_target_pairs={{0,8},{8,0},{1,9},{9,1},{2,10},{10,2},{3,11},{11,3},{4,12},{12,4},... | collective-permute-start | bytes 1572872 | tf_op jit(solution)/shard_map/ppermute | solution.py:16
  159.5 26.8 %collective-permute-start.4 = (bf16[512,512]{0,1:T(8,128)(2,1)S(1)}, bf16[512,512]{0,1:T(8,128)(2,1)S(1)}, u32[]{:S(2)}, u32[]{:S(2)}) collective-permute-start(bf16[512,512]{0,1:T(8,128)(2,1)S(1)} %get-tuple-element.21), channel_id=1, source_target_pairs={{0,16},{16,0},{1,17},{17,1},{2,18},{18,2},{3,19},{19,3},{4,20},{20... | collective-permute-start | bytes 1572872 | tf_op jit(solution)/shard_map/ppermute | solution.py:16
  186.3 64.3 %copy-start.2 = (bf16[512,512]{0,1:T(8,128)(2,1)}, bf16[512,512]{0,1:T(8,128)(2,1)S(1)}, u32[]{:S(2)}) copy-start(bf16[512,512]{0,1:T(8,128)(2,1)S(1)} %collective-permute-done.4) | copy-start | bytes 1572868
  186.3 75.7 %copy-start.4 = (bf16[256,512]{1,0:T(8,128)(2,1)S(1)}, bf16[256,512]{1,0:T(8,128)(2,1)}, u32[]{:S(2)}) copy-start(bf16[256,512]{1,0:T(8,128)(2,1)} %reduce-scatter.2.cloned.1.call-done) | copy-start | bytes 786436
  186.5 63.9 %collective-permute-start.5 = (bf16[512,512]{0,1:T(8,128)(2,1)S(1)}, bf16[512,512]{0,1:T(8,128)(2,1)S(1)}, u32[]{:S(2)}, u32[]{:S(2)}) collective-permute-start(bf16[512,512]{0,1:T(8,128)(2,1)S(1)} %fusion.6), channel_id=1, source_target_pairs={{0,32},{32,0},{1,33},{33,1},{2,34},{34,2},{3,35},{35,3},{4,36},{36... | collective-permute-start | bytes 1572872 | tf_op jit(solution)/shard_map/ppermute | solution.py:16
  250.4 12.5 %copy-start.5 = (bf16[512,512]{0,1:T(8,128)(2,1)}, bf16[512,512]{0,1:T(8,128)(2,1)S(1)}, u32[]{:S(2)}) copy-start(bf16[512,512]{0,1:T(8,128)(2,1)S(1)} %collective-permute-done.5) | copy-start | bytes 1572868
  250.6 32.0 %collective-permute-start.6 = (bf16[512,512]{0,1:T(8,128)(2,1)S(1)}, bf16[512,512]{0,1:T(8,128)(2,1)}, u32[]{:S(2)}, u32[]{:S(2)}) collective-permute-start(bf16[512,512]{0,1:T(8,128)(2,1)S(1)} %fusion.8), channel_id=1, source_target_pairs={{0,64},{64,0},{1,65},{65,1},{2,66},{66,2},{3,67},{67,3},{4,68},{68... | collective-permute-start | bytes 1572872 | tf_op jit(solution)/shard_map/ppermute | solution.py:16
  284.8 1.0 copy-start.3
Sparse Core Ops, SparseCore 0:
  10.9 34.3 reduce-scatter.1
  47.7 58.1 all-reduce.2
where the time goes:
time: 444 us; the launch traced here: 437 us
  waiting for transfers between devices  226 us (51%)
  other arithmetic  126 us (28%)
  starting transfers between devices  38.8 us (9%)
  between operations  16.2 us (4%)
  matrix products  15.6 us (4%)
  local copies, waits for them, and re-layouts  13.9 us (3%)
    ppermute x7, waiting for transfers between devices, from_partner(): return lax.ppermute(block, axis, route)  133 us
    another operation x14, other arithmetic, body(): lower_factor = jnp.linalg.cholesky(merged_gram)  78.8 us
    psum x1, waiting for transfers between devices, body(): lax.psum(column_gram(sketched).astype(jnp.bfloat16), 'dir')  58.5 us
    another operation x3, other arithmetic, right_solve(): lax.linalg.triangular_solve(lower_factor, matrix, left_side=False, lower=...  40.3 us
    ppermute x7, starting transfers between devices, from_partner(): return lax.ppermute(block, axis, route)  38.8 us
    reduce_scatter x1, waiting for transfers between devices, body(): lax.psum_scatter(jnp.dot(scaled_values, sketch, preferred_element_type=jn...  34.5 us
    another operation x12, local copies, waits for them, and re-layouts  10.5 us
  transfers between devices with their start and end apart: 9, of which 9 were waited for; matrix products, arithmetic and copies ran while one was open for 0% of the time, Pallas kernels for 0%

commit v1 on v0

v1 whole, which is shorter than its diff:
```python
import math

import jax
import jax.numpy as jnp
from jax import lax
from jax.sharding import Mesh, PartitionSpec as P

TILE = 128
PLANE = ("dir", "y", "core")


def scales_of(exponent_table):
    total = jnp.zeros(exponent_table.shape, jnp.float32)
    for exponent_value in range(-2, 3):
        total = total + jnp.where(
            exponent_table == exponent_value, jnp.float32(2.0**exponent_value), jnp.float32(0.0)
        )
    return total.astype(jnp.bfloat16)


def dequantize(values, exponent_table):
    height, breadth = values.shape
    edge_rows = height // exponent_table.shape[0]
    edge_cols = breadth // exponent_table.shape[1]
    scale_table = scales_of(exponent_table)
    tiled = values.reshape(exponent_table.shape[0], edge_rows, exponent_table.shape[1], edge_cols)
    tiled = tiled * scale_table[:, None, :, None]
    return tiled.reshape(height, breadth)


def right_solve(lower_factor, matrix):
    return lax.linalg.triangular_solve(
        lower_factor, matrix, left_side=False, lower=True, transpose_a=True
    )


def sum_of(pieces):
    return jnp.sum(pieces.astype(jnp.float32), axis=0)


def copies(piece, count):
    return jnp.broadcast_to(piece[None], (count,) + piece.shape)


def body(slab, exponents, sketch):
    scaled_values = dequantize(slab, exponents)
    partial_values = jnp.dot(scaled_values, sketch, preferred_element_type=jnp.float32)
    dirs = lax.axis_size("dir")
    rank = sketch.shape[1]
    parts = partial_values.astype(jnp.bfloat16).reshape(dirs, -1, rank)
    sketched = sum_of(lax.all_to_all(parts, "dir", 0, 0))

    rounded = sketched.astype(jnp.bfloat16)
    tiles = rank // TILE
    rows = []
    for i in range(tiles):
        rows.append(
            lax.dot_general(
                rounded[:, i * TILE : (i + 1) * TILE],
                rounded[:, i * TILE :],
                (((0,), (0,)), ((), ())),
                preferred_element_type=jnp.float32,
            ).astype(jnp.bfloat16)
        )
    blocks = [
        rows[i][:, (j - i) * TILE : (j - i + 1) * TILE] for i in range(tiles) for j in range(i, tiles)
    ]
    planes = lax.axis_size(PLANE)
    pieces = jnp.concatenate(blocks, axis=0).reshape(planes, -1, TILE)
    mine = sum_of(lax.all_to_all(pieces, PLANE, 0, 0)).astype(jnp.bfloat16)
    mine = sum_of(lax.all_to_all(copies(mine, lax.axis_size("z")), "z", 0, 0)).astype(jnp.bfloat16)
    merged = lax.all_to_all(copies(mine, planes), PLANE, 0, 0).reshape(-1, TILE, TILE)
    merged = merged.astype(jnp.float32)

    grid = [[None] * tiles for _ in range(tiles)]
    at = 0
    for i in range(tiles):
        for j in range(i, tiles):
            grid[i][j] = merged[at]
            grid[j][i] = merged[at].T
            at += 1
    gram = jnp.block(grid)
    lower_factor = jnp.linalg.cholesky(gram, symmetrize_input=False)
    orthonormal = right_solve(lower_factor, sketched)
    texel_count = sketched.shape[0] * lax.axis_size(("dir", "z", "y", "core"))
    return (orthonormal * math.sqrt(texel_count)).astype(jnp.bfloat16)


def solution(mesh):
    fine = Mesh(mesh.devices.reshape(4, 16, 4, 2), ("dir", "z", "y", "core"))
    tex = ("z", "y", "core")
    return jax.shard_map(
        body,
        mesh=fine,
        in_specs=(P(tex, "dir"), P(tex, "dir"), P("dir", None)),
        out_specs=P(tex + ("dir",), None),
        check_vma=False,
    )
```

time: 444 us -> 233 us (0.52); the launches traced: 437 us -> 233 us
  waiting for transfers between devices: 226 us -> 9.45 us
  blocking collectives: 0 us -> 63 us
  starting transfers between devices: 38.8 us -> 6.65 us
  between operations: 16.2 us -> 2.92 us
    ppermute x7 -> x0, waiting for transfers between devices: 133 us -> none  [from_partner(): return lax.ppermute(block, axis, route)]
    all_to_all x0 -> x3, blocking collectives: none -> 63 us  [the longest x1 27.6 us: body(): lax.all_to_all(copies(mine, lax.axis_size('z')), 'z', 0, 0)]
    psum x1 -> x0, waiting for transfers between devices: 58.5 us -> none  [body(): lax.psum(column_gram(sketched).astype(jnp.bfloat16), 'dir')]
    ppermute x7 -> x0, starting transfers between devices: 38.8 us -> none  [from_partner(): return lax.ppermute(block, axis, route)]
    reduce_scatter x1 -> x0, waiting for transfers between devices: 34.5 us -> none  [body(): lax.psum_scatter(jnp.dot(scaled_values, sketch, preferred_element_type=jn...]
    all_to_all x0 -> x1, waiting for transfers between devices: none -> 9.45 us  [body(): lax.all_to_all(copies(mine, planes), PLANE, 0, 0).reshape(-1, TILE, TILE)]
    all_to_all x0 -> x1, starting transfers between devices: none -> 6.65 us  [body(): lax.all_to_all(copies(mine, planes), PLANE, 0, 0).reshape(-1, TILE, TILE)]
    another operation x16 -> x15, local copies, waits for them, and re-layouts: 10.6 us -> 13.8 us
  transfers between devices with their start and end apart: 9 -> 1, of which waited for: 9 -> 1; matrix products, arithmetic and copies ran while one was open for 0% -> 0% of each run, Pallas kernels for 0% -> 0%
where the time goes in v1:
time: 233 us
  other arithmetic  122 us (52%)
  blocking collectives  63 us (27%)
  local copies, waits for them, and re-layouts  17.6 us (8%)
  matrix products  11.4 us (5%)
  waiting for transfers between devices  9.45 us (4%)
  starting transfers between devices  6.65 us (3%)
  between operations  2.92 us (1%)
    another operation x14, other arithmetic, body(): lower_factor = jnp.linalg.cholesky(gram, symmetrize_input=False)  79.3 us
    another operation x3, other arithmetic, right_solve(): lax.linalg.triangular_solve(lower_factor, matrix, left_side=False, lower=...  41.2 us
    all_to_all x1, blocking collectives, body(): lax.all_to_all(copies(mine, lax.axis_size('z')), 'z', 0, 0)  27.6 us
    all_to_all x1, blocking collectives, body(): mine = sum_of(lax.all_to_all(pieces, PLANE, 0, 0)).astype(jnp.bfloat16)  20.3 us
    all_to_all x1, blocking collectives, body(): sketched = sum_of(lax.all_to_all(parts, 'dir', 0, 0))  15.1 us
    another operation x12, local copies, waits for them, and re-layouts  13.7 us
    all_to_all x1, waiting for transfers between devices, body(): lax.all_to_all(copies(mine, planes), PLANE, 0, 0).reshape(-1, TILE, TILE)  9.45 us
    all_to_all x1, starting transfers between devices, body(): lax.all_to_all(copies(mine, planes), PLANE, 0, 0).reshape(-1, TILE, TILE)  6.65 us
  transfers between devices with their start and end apart: 1, of which 1 were waited for; matrix products, arithmetic and copies ran while one was open for 0% of the time, Pallas kernels for 0%

profile of v1, /device:TPU:1, one launch (start us, length us, event | category | flops | bytes accessed | tf_op | source)
XLA Modules:
  0.0 232.7 jit_solution(11586496054677551037)
XLA Ops:
  0.0 0.8 add_convert_fusion
  0.8 0.3 mul.17
  1.2 0.7 copy-done.2
  1.9 1.2 fusion.2
  3.2 15.1 %all_to_all.20 = bf16[4,256,512]{2,1,0:T(8,128)(2,1)S(1)} all-to-all(bf16[4,256,512]{2,1,0:T(8,128)(2,1)S(1)} %bitcast.105), channel_id=1, replica_groups=mesh['dir'=4,'z'=16,'y'=4,'core'=2] {'dir'}, dimensions={0} | all-to-all | bytes 2097152 | tf_op jit(solution)/shard_map/all_to_all | solution.py:51
  18.5 0.2 convolution_convert_fusion
  18.7 0.2 convolution_convert_fusion.1
  19.3 0.2 fusion.3
  19.5 20.3 %all_to_all.21 = bf16[32,40,128]{2,1,0:T(8,128)(2,1)S(1)} all-to-all(bf16[32,40,128]{2,1,0:T(8,128)(2,1)S(1)} %bitcast.106), channel_id=1, replica_groups=mesh['dir'=4,'z'=16,'y'=4,'core'=2] {'dir','y','core'}, dimensions={0} | all-to-all | bytes 655360 | tf_op jit(solution)/shard_map/all_to_all | solution.py:70
  39.8 27.6 %all_to_all.22 = bf16[16,40,128]{2,1,0:T(8,128)(2,1)S(1)} all-to-all(bf16[16,40,128]{2,1,0:T(8,128)(2,1)S(1)} %broadcast_in_dim.45), channel_id=1, replica_groups=mesh['dir'=4,'z'=16,'y'=4,'core'=2] {'z'}, dimensions={0} | all-to-all | bytes 327680 | tf_op jit(solution)/shard_map/all_to_all | solution.py:71
  67.5 0.8 broadcast_in_dim.46
  68.2 6.6 %all-to-all-start.3 = ((bf16[32,40,128]{2,1,0:T(8,128)(2,1)}), bf16[32,40,128]{2,1,0:T(8,128)(2,1)S(1)}, u32[]{:S(2)}, u32[]{:S(2)}) async-start(bf16[32,40,128]{2,1,0:T(8,128)(2,1)} %broadcast_in_dim.46), calls=%async_computation.3 | async-start | bytes 655360 | tf_op jit(solution)/shard_map/all_to_all | solution.py:72
  74.9 9.4 %all-to-all-done.3 = bf16[32,40,128]{2,1,0:T(8,128)(2,1)S(1)} async-done(((bf16[32,40,128]{2,1,0:T(8,128)(2,1)}), bf16[32,40,128]{2,1,0:T(8,128)(2,1)S(1)}, u32[]{:S(2)}, u32[]{:S(2)}) %all-to-all-start.3) | async-done | bytes 327712 | tf_op jit(solution)/shard_map/all_to_all | solution.py:72
  84.7 11.7 %cholesky.101 = f32[128,128]{1,0:T(8,128)S(1)} custom-call(f32[128,128]{1,0:T(8,128)S(1)} %copy.15), custom_call_target="Cholesky" | custom-call | tf_op jit(solution)/shard_map/jit(cholesky)/cholesky | solution.py:83
  96.4 10.4 %custom-call.30 = f32[1,128,128]{1,2,0:T(8,128)} custom-call(f32[1,128,128]{2,1,0:T(8,128)S(1)} %get-tuple-element.45), custom_call_target="InvertDiagBlocksLowerTriangular" | custom-call | tf_op jit(solution)/shard_map/jit(cholesky)/cholesky | solution.py:83
  107.8 1.2 constant_dynamic-update-slice_fusion.3
  109.0 1.2 convolution_subtract_fusion
  110.2 11.7 %cholesky.212 = f32[128,128]{1,0:T(8,128)S(1)} custom-call(f32[128,128]{1,0:T(8,128)S(1)} %cholesky.261), custom_call_target="Cholesky" | custom-call | tf_op jit(solution)/shard_map/jit(cholesky)/cholesky | solution.py:83
  121.9 10.0 %custom-call.31 = f32[1,128,128]{1,2,0:T(8,128)S(1)} custom-call(f32[1,128,128]{2,1,0:T(8,128)S(1)} %get-tuple-element.42), custom_call_target="InvertDiagBlocksLowerTriangular" | custom-call | tf_op jit(solution)/shard_map/jit(cholesky)/cholesky | solution.py:83
  131.9 0.3 convolution_dynamic-update-slice_fusion
  132.2 0.4 convolution_subtract_fusion.3
  132.6 11.7 %cholesky.233 = f32[128,128]{1,0:T(8,128)S(1)} custom-call(f32[128,128]{1,0:T(8,128)S(1)} %cholesky.265), custom_call_target="Cholesky" | custom-call | tf_op jit(solution)/shard_map/jit(cholesky)/cholesky | solution.py:83
  144.4 0.7 compare_reduce_fusion.1
  145.1 9.8 %custom-call.32 = f32[1,128,128]{1,2,0:T(8,128)S(1)} custom-call(f32[1,128,128]{2,1,0:T(8,128)S(1)} %get-tuple-element.39), custom_call_target="InvertDiagBlocksLowerTriangular" | custom-call | tf_op jit(solution)/shard_map/jit(cholesky)/cholesky | solution.py:83
  154.9 0.2 convolution_dynamic-update-slice_fusion.1
  155.1 0.4 convolution_subtract_fusion.5
  155.5 11.7 %cholesky.249 = f32[128,128]{1,0:T(8,128)S(1)} custom-call(f32[128,128]{1,0:T(8,128)S(1)} %convolution_subtract_fusion.5), custom_call_target="Cholesky" | custom-call | tf_op jit(solution)/shard_map/jit(cholesky)/cholesky | solution.py:83
  167.2 0.6 compare_reduce_fusion
  167.9 0.7 compare_reduce_fusion.2
  171.1 1.1 select_select_fusion
  172.2 13.7 %while.1 = (s32[]{:T(128)}, f32[512,512]{1,0:T(8,128)}, s32[4,2]{0,1:T(2,128)S(1)}, f32[4,128,128]{2,1,0:T(8,128)}, s32[]{:T(128)}) while((s32[]{:T(128)}, f32[512,512]{1,0:T(8,128)}, s32[4,2]{0,1:T(2,128)S(1)}, f32[4,128,128]{2,1,0:T(8,128)}, s32[]{:T(128)}) %tuple.39), condition=%wide.while_cond, body=%wide.while_body.sunk | while | flops 2 | bytes 132705 | solution.py:32
  172.3 0.5 fusion.57
  172.8 2.8 %bitcast_dynamic-update-slice_fusion.2 = f32[4,128,128]{2,1,0:T(8,128)} fusion(f32[4,128,128]{2,1,0:T(8,128)} %get-tuple-element.87, s32[]{:T(128)} %get-tuple-element.84, f32[512,512]{1,0:T(8,128)} %get-tuple-element.90, s32[]{:T(128)} %bitcast.98, s32[]{:T(128)} %bitcast.99), kind=kLoop, calls=%fused_computation.clone.1 | loop fusion | bytes 132608 | tf_op jit(solution)/shard_map/triangular_solve
  175.7 0.5 fusion.57
  176.3 2.8 %bitcast_dynamic-update-slice_fusion.2 = f32[4,128,128]{2,1,0:T(8,128)} fusion(f32[4,128,128]{2,1,0:T(8,128)} %get-tuple-element.87, s32[]{:T(128)} %get-tuple-element.84, f32[512,512]{1,0:T(8,128)} %get-tuple-element.90, s32[]{:T(128)} %bitcast.98, s32[]{:T(128)} %bitcast.99), kind=kLoop, calls=%fused_computation.clone.1 | loop fusion | bytes 132608 | tf_op jit(solution)/shard_map/triangular_solve
  179.2 0.5 fusion.57
  179.7 2.8 %bitcast_dynamic-update-slice_fusion.2 = f32[4,128,128]{2,1,0:T(8,128)} fusion(f32[4,128,128]{2,1,0:T(8,128)} %get-tuple-element.87, s32[]{:T(128)} %get-tuple-element.84, f32[512,512]{1,0:T(8,128)} %get-tuple-element.90, s32[]{:T(128)} %bitcast.98, s32[]{:T(128)} %bitcast.99), kind=kLoop, calls=%fused_computation.clone.1 | loop fusion | bytes 132608 | tf_op jit(solution)/shard_map/triangular_solve
  182.6 0.5 fusion.57
  183.2 2.8 %bitcast_dynamic-update-slice_fusion.2 = f32[4,128,128]{2,1,0:T(8,128)} fusion(f32[4,128,128]{2,1,0:T(8,128)} %get-tuple-element.87, s32[]{:T(128)} %get-tuple-element.84, f32[512,512]{1,0:T(8,128)} %get-tuple-element.90, s32[]{:T(128)} %bitcast.98, s32[]{:T(128)} %bitcast.99), kind=kLoop, calls=%fused_computation.clone.1 | loop fusion | bytes 132608 | tf_op jit(solution)/shard_map/triangular_solve
  185.9 40.1 %custom-call.33 = f32[4,128,128]{1,2,0:T(8,128)S(1)} custom-call(f32[4,128,128]{2,1,0:T(8,128)} %get-tuple-element.12), custom_call_target="InvertDiagBlocksLowerTriangular" | custom-call | tf_op jit(solution)/shard_map/triangular_solve | solution.py:32
  226.1 0.3 fusion.30
  226.4 1.2 convolution_subtract_fusion.4
  227.6 0.3 fusion.34
  227.9 1.5 convolution_subtract_fusion.2
  229.4 0.3 fusion.33
  229.8 1.8 convolution_subtract_fusion.1
  231.5 0.3 fusion.32
  231.9 0.8 copy.25
  (47 shorter events, 2.3 us)
Async XLA Ops:
  0.0 1.2 copy-start
  0.0 1.9 copy-start.2
  68.2 16.1 %all-to-all-start.3 = ((bf16[32,40,128]{2,1,0:T(8,128)(2,1)}), bf16[32,40,128]{2,1,0:T(8,128)(2,1)S(1)}, u32[]{:S(2)}, u32[]{:S(2)}) async-start(bf16[32,40,128]{2,1,0:T(8,128)(2,1)} %broadcast_in_dim.46), calls=%async_computation.3 | async-start | bytes 655360 | tf_op jit(solution)/shard_map/all_to_all | solution.py:72
  107.8 1.2 copy-start.1

commit v2 on v1

--- a/solution.py
+++ b/solution.py
@@ -1,11 +1,135 @@
+import functools
 import math
 
 import jax
 import jax.numpy as jnp
 from jax import lax
+from jax.experimental import pallas as pl
+from jax.experimental.pallas import tpu as pltpu
 from jax.sharding import Mesh, PartitionSpec as P
 
-TILE = 128
+f32=jnp.float32; bf=jnp.bfloat16
+TILE=128; PAN=8
+
+def halves(x):
+    hi=x.astype(bf)
+    return hi,(x-hi.astype(f32)).astype(bf)
+
+def product(a,b,dims):
+    (ah,al),(bh,bl)=a,b
+    def dot(x,y):
+        return lax.dot_general(x,y,(dims,((),())),preferred_element_type=f32)
+    return dot(ah,bh)+(dot(ah,bl)+dot(al,bh))
+
+def reciprocal(d):
+    r=pl.reciprocal(d,approx=True)
+    return r*(2.0-d*r)
+
+def spread_rows(x):
+    return [jnp.broadcast_to(x[i:i+1,:],x.shape) for i in range(PAN)]
+
+def factor(a_ref, u_ref, aside):
+    shape=(PAN,TILE)
+    sub=lax.broadcasted_iota(jnp.int32,shape,0)
+    lane=lax.broadcasted_iota(jnp.int32,shape,1)
+    pa=a_ref[0:PAN,0:TILE]; pm=a_ref[0:PAN,TILE:2*TILE]
+    steps=TILE//PAN
+    for p in range(steps):
+        c0=PAN*p
+        last=p==steps-1
+        columns=[jnp.broadcast_to(pa[:,c0+j:c0+j+1],shape) for j in range(PAN)]
+        e=[[jnp.broadcast_to(columns[j][i:i+1,:],shape) if i>=j else None for j in range(PAN)] for i in range(PAN)]
+        ua=spread_rows(pa); um=spread_rows(pm)
+        if not last:
+            cn=[jnp.broadcast_to(jnp.sum(jnp.where(lane==c0+PAN+sub,ua[j],0.0),axis=1,keepdims=True),shape) for j in range(PAN)]
+        inv=[None]*PAN
+        for j in range(PAN):
+            inv[j]=reciprocal(e[j][j])
+            for i in range(j+1,PAN):
+                l=e[i][j]*inv[j]
+                for k in range(j+1,i+1):
+                    e[i][k]=e[i][k]-l*e[k][j]
+                ua[i]=ua[i]-l*ua[j]
+                um[i]=um[i]-l*um[j]
+                if not last: cn[i]=cn[i]-l*cn[j]
+        outa=jnp.zeros(shape,f32); outm=jnp.zeros(shape,f32)
+        for i in range(PAN):
+            rs=lax.rsqrt(e[i][i])
+            outa=jnp.where(sub==i,ua[i]*rs,outa)
+            outm=jnp.where(sub==i,um[i]*rs,outm)
+        u_ref[c0:c0+PAN,:]=outm
+        if aside: aside.pop(0)()
+        if not last:
+            pa=a_ref[c0+PAN:c0+2*PAN,0:TILE]; pm=a_ref[c0+PAN:c0+2*PAN,TILE:2*TILE]
+            for j in range(PAN):
+                w=cn[j]*inv[j]
+                pa=pa-w*ua[j]; pm=pm-w*um[j]
+            r0=c0+2*PAN
+            if r0<TILE:
+                al=outa-outa.astype(bf).astype(f32); ml=outm-outm.astype(bf).astype(f32)
+                lhs=jnp.concatenate([outa,outa,al],axis=0).astype(bf)
+                hi=jnp.concatenate([outa,outm],axis=1)
+                lo=jnp.concatenate([al,ml],axis=1)
+                rhs=jnp.concatenate([hi,lo,hi],axis=0).astype(bf)
+                upd=lax.dot_general(lhs,rhs,(((0,),(0,)),((),())),preferred_element_type=f32)
+                a_ref[r0:TILE,:]=a_ref[r0:TILE,:]-upd[r0:TILE,:]
+    while aside: aside.pop(0)()
+
+NN=((1,),(0,)); TN=((0,),(0,)); NT=((1,),(1,))
+
+def whiten_kernel(scale, gram_ref, s_ref, out_ref, a_ref, r_ref, f_ref, w_ref, uh_ref, ul_ref):
+    rank=s_ref.shape[1]; tiles=rank//TILE
+    cut=lambda i: slice(i*TILE,(i+1)*TILE)
+    row=lax.broadcasted_iota(jnp.int32,(TILE,TILE),0); col=lax.broadcasted_iota(jnp.int32,(TILE,TILE),1)
+    eye=jnp.where(row==col,1.0,0.0)
+    at=0
+    for i in range(tiles):
+        for j in range(i,tiles):
+            blk=gram_ref[at*TILE:(at+1)*TILE,:].astype(f32)
+            if i==j==0: f_ref[:,0:TILE]=blk
+            else: a_ref[cut(i),cut(j)]=blk
+            at+=1
+    r_ref[...]=s_ref[...].astype(f32)
+    aside=[]
+    for k in range(tiles):
+        f_ref[:,TILE:2*TILE]=eye
+        factor(f_ref,w_ref,aside)
+        w=halves(w_ref[...])
+        rest=slice((k+1)*TILE,rank)
+        aside=[]
+        if k<tiles-1:
+            u=halves(product(w,halves(a_ref[cut(k),rest]),NN))
+            uh_ref[cut(k),rest]=u[0]; ul_ref[cut(k),rest]=u[1]
+            first=(u[0][:,0:TILE],u[1][:,0:TILE])
+            f_ref[:,0:TILE]=a_ref[cut(k+1),cut(k+1)]-product(first,first,TN)
+        def solve(k=k,w=w):
+            q=product(halves(r_ref[:,cut(k)]),w,NT)
+            out_ref[:,cut(k)]=(q*scale).astype(out_ref.dtype)
+            if k<tiles-1: r_ref[:,cut(k)]=q
+        def trail(i,lo,k=k):
+            def run():
+                a=(uh_ref[cut(k),cut(i)],ul_ref[cut(k),cut(i)])
+                b=(uh_ref[cut(k),lo*TILE:rank],ul_ref[cut(k),lo*TILE:rank])
+                a_ref[cut(i),lo*TILE:rank]=a_ref[cut(i),lo*TILE:rank]-product(a,b,TN)
+            return run
+        def carry(i,k=k):
+            def run():
+                u=(uh_ref[cut(k),cut(i)],ul_ref[cut(k),cut(i)])
+                r_ref[:,cut(i)]=r_ref[:,cut(i)]-product(halves(r_ref[:,cut(k)]),u,NN)
+            return run
+        if k<tiles-1:
+            if k+2<tiles: aside.append(trail(k+1,k+2))
+            for i in range(k+2,tiles): aside.append(trail(i,i))
+            aside.append(solve)
+            for i in range(k+1,tiles): aside.append(carry(i))
+        else: solve()
+
+def whiten(gram,s,scale):
+    rows,rank=s.shape
+    return pl.pallas_call(functools.partial(whiten_kernel,scale),out_shape=jax.ShapeDtypeStruct((rows,rank),bf),
+        scratch_shapes=[pltpu.VMEM((rank,rank),f32),pltpu.VMEM((rows,rank),f32),pltpu.VMEM((TILE,2*TILE),f32),pltpu.VMEM((TILE,TILE),f32),pltpu.VMEM((rank,rank),bf),pltpu.VMEM((rank,rank),bf)],
+        compiler_params=pltpu.CompilerParams(vmem_limit_bytes=32*1024*1024),)(gram,s)
+
 PLANE = ("dir", "y", "core")
 
 
@@ -26,12 +150,6 @@
     tiled = values.reshape(exponent_table.shape[0], edge_rows, exponent_table.shape[1], edge_cols)
     tiled = tiled * scale_table[:, None, :, None]
     return tiled.reshape(height, breadth)
-
-
-def right_solve(lower_factor, matrix):
-    return lax.linalg.triangular_solve(
-        lower_factor, matrix, left_side=False, lower=True, transpose_a=True
-    )
 
 
 def sum_of(pieces):
@@ -69,21 +187,9 @@
     pieces = jnp.concatenate(blocks, axis=0).reshape(planes, -1, TILE)
     mine = sum_of(lax.all_to_all(pieces, PLANE, 0, 0)).astype(jnp.bfloat16)
     mine = sum_of(lax.all_to_all(copies(mine, lax.axis_size("z")), "z", 0, 0)).astype(jnp.bfloat16)
-    merged = lax.all_to_all(copies(mine, planes), PLANE, 0, 0).reshape(-1, TILE, TILE)
-    merged = merged.astype(jnp.float32)
-
-    grid = [[None] * tiles for _ in range(tiles)]
-    at = 0
-    for i in range(tiles):
-        for j in range(i, tiles):
-            grid[i][j] = merged[at]
-            grid[j][i] = merged[at].T
-            at += 1
-    gram = jnp.block(grid)
-    lower_factor = jnp.linalg.cholesky(gram, symmetrize_input=False)
-    orthonormal = right_solve(lower_factor, sketched)
+    merged = lax.all_to_all(copies(mine, planes), PLANE, 0, 0).reshape(-1, TILE)
     texel_count = sketched.shape[0] * lax.axis_size(("dir", "z", "y", "core"))
-    return (orthonormal * math.sqrt(texel_count)).astype(jnp.bfloat16)
+    return whiten(merged, rounded, math.sqrt(texel_count))
 
 
 def solution(mesh):

time: 233 us -> 99.4 us (0.43)
  other arithmetic: 122 us -> 1.18 us
  local copies, waits for them, and re-layouts: 17.6 us -> 1.25 us
  blocking collectives: 63 us -> 78.9 us
  Pallas kernels: 0 us -> 15.6 us
  waiting for transfers between devices: 9.45 us -> 0 us
  matrix products: 11.4 us -> 2.06 us
  starting transfers between devices: 6.65 us -> 0 us
  between operations: 2.92 us -> 0.11 us
    another operation x17 -> x0, other arithmetic: 121 us -> none  [the longest x14 79.3 us: body(): lower_factor = jnp.linalg.cholesky(gram, symmetrize_input=False)]
    all_to_all x0 -> x1, blocking collectives: none -> 15.9 us  [body(): merged = lax.all_to_all(copies(mine, planes), PLANE, 0, 0).reshape(-1, TILE)]
    pallas_call x0 -> x1, Pallas kernels: none -> 15.6 us  [whiten(): pl.pallas_call(functools.partial(whiten_kernel, scale), out_shape=jax.Sha...]
    another operation x16 -> x0, local copies, waits for them, and re-layouts: 13.8 us -> none
    all_to_all x1 -> x0, waiting for transfers between devices: 9.45 us -> none  [body(): lax.all_to_all(copies(mine, planes), PLANE, 0, 0).reshape(-1, TILE, TILE)]
    another operation x13 -> x0, matrix products: 9.32 us -> none  [the longest x7 5.74 us: right_solve(): lax.linalg.triangular_solve(lower_factor, matrix, left_side=False, lower=...]
    all_to_all x1 -> x0, starting transfers between devices: 6.65 us -> none  [body(): lax.all_to_all(copies(mine, planes), PLANE, 0, 0).reshape(-1, TILE, TILE)]
  transfers between devices with their start and end apart: 1 -> 0, of which waited for: 1 -> 0; matrix products, arithmetic and copies ran while one was open for 0% -> 0% of each run, Pallas kernels for 0% -> 0%
where the time goes in v2:
time: 99.4 us; the launch traced here: 99.1 us
  blocking collectives  78.9 us (79%)
  Pallas kernels  15.6 us (16%)
  matrix products  2.06 us (2%)
  local copies, waits for them, and re-layouts  1.25 us (1%)
  other arithmetic  1.18 us (1%)
    all_to_all x1, blocking collectives, body(): lax.all_to_all(copies(mine, lax.axis_size('z')), 'z', 0, 0)  27.6 us
    all_to_all x1, blocking collectives, body(): mine = sum_of(lax.all_to_all(pieces, PLANE, 0, 0)).astype(jnp.bfloat16)  20.3 us
    all_to_all x1, blocking collectives, body(): merged = lax.all_to_all(copies(mine, planes), PLANE, 0, 0).reshape(-1, TILE)  15.9 us
    pallas_call x1, Pallas kernels, whiten(): pl.pallas_call(functools.partial(whiten_kernel, scale), out_shape=jax.Sha...  15.6 us
    all_to_all x1, blocking collectives, body(): sketched = sum_of(lax.all_to_all(parts, 'dir', 0, 0))  15.1 us

profile of v2, /device:TPU:1, one launch (start us, length us, event | category | flops | bytes accessed | tf_op | source)
XLA Modules:
  0.0 99.1 jit_solution(14638861887406904880)
XLA Ops:
  0.0 0.0 copy-start
  0.0 0.0 copy-start.1
  0.0 0.8 add_convert_fusion
  0.8 0.3 mul.11
  1.2 0.0 copy-done
  1.2 0.7 copy-done.1
  1.9 1.2 %fusion.2 = bf16[1024,512]{1,0:T(8,128)(2,1)S(1)} fusion(bf16[1024,512]{1,0:T(8,128)(2,1)S(1)} %copy-done, bf16[1024,1024]{1,0:T(8,128)(2,1)S(1)} %copy-done.1, bf16[128,8,8,128]{3,2,1,0:T(8,128)(2,1)S(1)} %bitcast.13), kind=kOutput, calls=%fused_computation.3 | convolution fusion | flops 1075314688 | bytes 6291456 | tf_op jit(solution)/shard_map/dot_general | solution.py:165
  3.2 15.1 %all_to_all.20 = bf16[4,256,512]{2,1,0:T(8,128)(2,1)S(1)} all-to-all(bf16[4,256,512]{2,1,0:T(8,128)(2,1)S(1)} %bitcast.14), channel_id=1, replica_groups=mesh['dir'=4,'z'=16,'y'=4,'core'=2] {'dir'}, dimensions={0} | all-to-all | bytes 2097152 | tf_op jit(solution)/shard_map/all_to_all | solution.py:169
  18.3 0.2 reduce_sum.36.s_ref
  18.5 0.2 convolution_convert_fusion.2
  18.7 0.2 convolution_convert_fusion.1
  19.0 0.2 convolution_convert_fusion
  19.3 0.2 fusion.3
  19.5 20.3 %all_to_all.21 = bf16[32,40,128]{2,1,0:T(8,128)(2,1)S(1)} all-to-all(bf16[32,40,128]{2,1,0:T(8,128)(2,1)S(1)} %bitcast.15), channel_id=1, replica_groups=mesh['dir'=4,'z'=16,'y'=4,'core'=2] {'dir','y','core'}, dimensions={0} | all-to-all | bytes 655360 | tf_op jit(solution)/shard_map/all_to_all | solution.py:188
  39.8 0.1 reduce_sum.37
  39.9 27.6 %all_to_all.22 = bf16[16,40,128]{2,1,0:T(8,128)(2,1)S(1)} all-to-all(bf16[16,40,128]{2,1,0:T(8,128)(2,1)S(1)} %broadcast_in_dim.43), channel_id=1, replica_groups=mesh['dir'=4,'z'=16,'y'=4,'core'=2] {'z'}, dimensions={0} | all-to-all | bytes 327680 | tf_op jit(solution)/shard_map/all_to_all | solution.py:189
  67.6 15.9 %all_to_all.23 = bf16[32,40,128]{2,1,0:T(8,128)(2,1)S(1)} all-to-all(bf16[32,40,128]{2,1,0:T(8,128)(2,1)S(1)} %broadcast_in_dim.44), channel_id=1, replica_groups=mesh['dir'=4,'z'=16,'y'=4,'core'=2] {'dir','y','core'}, dimensions={0} | all-to-all | bytes 655360 | tf_op jit(solution)/shard_map/all_to_all | solution.py:190
  83.5 15.6 %shard_map.37 = bf16[256,512]{1,0:T(8,128)(2,1)} custom-call(bf16[1280,128]{1,0:T(8,128)(2,1)S(1)} %bitcast.12, bf16[256,512]{1,0:T(8,128)(2,1)S(1)} %reduce_sum.36.s_ref), custom_call_target="tpu_custom_call" | custom-call | tf_op jit(solution)/shard_map/pallas_call | solution.py:129
  (12 shorter events, 0.2 us)
Async XLA Ops:
  0.0 1.2 %copy-start = (bf16[1024,512]{1,0:T(8,128)(2,1)S(1)}, bf16[1024,512]{1,0:T(8,128)(2,1)}, u32[]{:S(2)}) copy-start(bf16[1024,512]{1,0:T(8,128)(2,1)} %param.5) | copy-start | bytes 3145732
  0.0 1.9 %copy-start.1 = (bf16[1024,1024]{1,0:T(8,128)(2,1)S(1)}, bf16[1024,1024]{1,0:T(8,128)(2,1)}, u32[]{:S(2)}) copy-start(bf16[1024,1024]{1,0:T(8,128)(2,1)} %param.3) | copy-start | bytes 6291460

commit v3 on v1

v3 whole, which is shorter than its diff:
```python
import functools
import math

import jax
import jax.numpy as jnp
import numpy as np
from jax import lax
from jax.experimental import pallas as pl
from jax.experimental.pallas import tpu as pltpu
from jax.sharding import Mesh, PartitionSpec as P

f32 = jnp.float32
bf16 = jnp.bfloat16
TILE = 128
PANEL = 8
NN = ((1,), (0,))
TN = ((0,), (0,))
NT = ((1,), (1,))


def cut(i):
    return slice(i * TILE, (i + 1) * TILE)


def halves(x):
    high = x.astype(bf16)
    return high, (x - high.astype(f32)).astype(bf16)


def product(a, b, dims):
    def dot(x, y):
        return lax.dot_general(x, y, (dims, ((), ())), preferred_element_type=f32)

    return dot(a[0], b[0]) + (dot(a[0], b[1]) + dot(a[1], b[0]))


def places():
    shape = (TILE, TILE)
    return lax.broadcasted_iota(jnp.int32, shape, 0), lax.broadcasted_iota(jnp.int32, shape, 1)


def tree(terms):
    while len(terms) > 1:
        odd = terms[len(terms) // 2 * 2 :]
        terms = [terms[i] + terms[i + 1] for i in range(0, len(terms) - 1, 2)] + odd
    return terms[0]


def factor(a_ref, w_ref, t_ref, aside):
    shape = (PANEL, TILE)
    sub = lax.broadcasted_iota(jnp.int32, shape, 0)
    lane = lax.broadcasted_iota(jnp.int32, shape, 1)
    steps = TILE // PANEL
    pa, pm = a_ref[0:PANEL, 0:TILE], a_ref[0:PANEL, TILE : 2 * TILE]
    for p in range(steps):
        at, after = p * PANEL, (p + 1) * PANEL
        base = p % 2 * PANEL * PANEL
        for j in range(PANEL):
            spread = jnp.broadcast_to(pa[:, at + j : at + j + 1], shape)
            t_ref[base + PANEL * j : base + PANEL * (j + 1), :] = spread
        e = [
            [t_ref[pl.ds(base + PANEL * j + i, PANEL, stride=0), :] for j in range(i + 1)]
            for i in range(PANEL)
        ]
        ua = [jnp.broadcast_to(pa[i : i + 1, :], shape) for i in range(PANEL)]
        um = [jnp.broadcast_to(pm[i : i + 1, :], shape) for i in range(PANEL)]
        more = p < steps - 1
        if more:
            here = lane == after + sub
            nxt = [
                jnp.broadcast_to(
                    jnp.sum(jnp.where(here, ua[j], 0.0), axis=1, keepdims=True), shape
                )
                for j in range(PANEL)
            ]
        inv = []
        for j in range(PANEL):
            inv.append(pl.reciprocal(e[j][j], approx=True))
            for i in range(j + 1, PANEL):
                ratio = e[i][j] * inv[j]
                for k in range(j + 1, i + 1):
                    e[i][k] = e[i][k] - ratio * e[k][j]
                ua[i] = ua[i] - ratio * ua[j]
                um[i] = um[i] - ratio * um[j]
                if more:
                    nxt[i] = nxt[i] - ratio * nxt[j]
        if more:
            weights = [nxt[j] * inv[j] for j in range(PANEL)]
            rows = slice(after, after + PANEL)
            pa = a_ref[rows, 0:TILE] - tree([w * u for w, u in zip(weights, ua)])
            pm = a_ref[rows, TILE : 2 * TILE] - tree([w * u for w, u in zip(weights, um)])
        outa, outm, pivots = ua[0], um[0], e[0][0]
        for i in range(1, PANEL):
            outa = jnp.where(sub == i, ua[i], outa)
            outm = jnp.where(sub == i, um[i], outm)
            pivots = jnp.where(sub == i, e[i][i], pivots)
        root = lax.rsqrt(pivots)
        outa, outm = outa * root, outm * root
        w_ref[at:after, :] = outm
        if aside:
            aside.pop(0)()
        rest = after + PANEL
        if rest < TILE:
            lowa = outa - outa.astype(bf16).astype(f32)
            lowm = outm - outm.astype(bf16).astype(f32)
            none = jnp.zeros(shape, f32)
            high = jnp.concatenate([outa, outm], axis=1)
            low = jnp.concatenate([lowa, lowm], axis=1)
            left = jnp.concatenate([outa, outa, lowa, none], axis=0).astype(bf16)
            right = jnp.concatenate([high, low, high, jnp.zeros_like(low)], axis=0).astype(bf16)
            update = lax.dot_general(left, right, (TN, ((), ())), preferred_element_type=f32)
            a_ref[rest:TILE, :] = a_ref[rest:TILE, :] - update[rest:TILE, :]
    while aside:
        aside.pop(0)()


def gram_kernel(parts_ref, s_ref, gram_ref):
    total = parts_ref[0].astype(f32)
    for g in range(1, parts_ref.shape[0]):
        total = total + parts_ref[g].astype(f32)
    s_ref[...] = total.astype(bf16)
    rank = s_ref.shape[1]
    tiles = rank // TILE
    row, col = places()
    at = tiles // 2
    diagonal = []
    for i in range(tiles):
        strip = lax.dot_general(
            s_ref[:, cut(i)],
            s_ref[:, i * TILE : rank],
            (TN, ((), ())),
            preferred_element_type=f32,
        )
        diagonal.append(strip[:, 0:TILE])
        for j in range(1, tiles - i):
            gram_ref[cut(at), :] = strip[:, cut(j)].astype(bf16)
            at += 1
    tail = []
    for i in range(0, tiles, 2):
        gram_ref[cut(i // 2), :] = jnp.where(col >= row, diagonal[i], diagonal[i + 1]).astype(bf16)
        tail.append(jnp.sum(jnp.where(row == col, diagonal[i + 1], 0.0), axis=0, keepdims=True))
    rest = gram_ref.shape[0] - at * TILE
    tail.append(jnp.zeros((rest - len(tail), TILE), f32))
    gram_ref[at * TILE : at * TILE + rest, :] = jnp.concatenate(tail, axis=0).astype(bf16)


def local_gram(parts, height):
    rows, rank = parts.shape[1:]
    return pl.pallas_call(
        gram_kernel,
        out_shape=(
            jax.ShapeDtypeStruct((rows, rank), bf16),
            jax.ShapeDtypeStruct((height, TILE), bf16),
        ),
        compiler_params=pltpu.CompilerParams(vmem_limit_bytes=32 * 1024 * 1024),
    )(parts)


def whiten_kernel(scale, gram_ref, s_ref, out_ref, a_ref, r_ref, f_ref, w_ref, t_ref, uh_ref, ul_ref):
    rank = s_ref.shape[1]
    tiles = rank // TILE
    row, col = places()
    eye = jnp.where(row == col, 1.0, 0.0)
    at = tiles // 2
    offset = tiles // 2 * TILE + tiles * (tiles - 1) // 2 * TILE
    tail = gram_ref[offset : offset + 16, :].astype(f32)
    for i in range(0, tiles, 2):
        pair = gram_ref[cut(i // 2), :].astype(f32)
        turned = jnp.transpose(pair)
        first = jnp.where(col >= row, pair, turned)
        second = jnp.where(col < row, pair, turned)
        second = jnp.where(row == col, tail[i // 2 : i // 2 + 1, :], second)
        if i == 0:
            f_ref[:, 0:TILE] = first
        else:
            a_ref[cut(i), cut(i)] = first
        a_ref[cut(i + 1), cut(i + 1)] = second
    for i in range(tiles):
        for j in range(i + 1, tiles):
            a_ref[cut(i), cut(j)] = gram_ref[cut(at), :].astype(f32)
            at += 1
    r_ref[...] = s_ref[...].astype(f32)
    aside = []
    for k in range(tiles):
        f_ref[:, TILE : 2 * TILE] = eye
        factor(f_ref, w_ref, t_ref, aside)
        w = halves(w_ref[...])
        aside = []
        last = k == tiles - 1
        if not last:
            rest = slice((k + 1) * TILE, rank)
            u = halves(product(w, halves(a_ref[cut(k), rest]), NN))
            uh_ref[cut(k), rest], ul_ref[cut(k), rest] = u
            near = (u[0][:, 0:TILE], u[1][:, 0:TILE])
            f_ref[:, 0:TILE] = a_ref[cut(k + 1), cut(k + 1)] - product(near, near, TN)

        def solve(k=k, w=w, last=last):
            q = product(halves(r_ref[:, cut(k)]), w, NT)
            out_ref[:, cut(k)] = (q * scale).astype(out_ref.dtype)
            if not last:
                r_ref[:, cut(k)] = q

        def trail(i, low, k=k):
            wide = slice(low * TILE, rank)
            a = (uh_ref[cut(k), cut(i)], ul_ref[cut(k), cut(i)])
            b = (uh_ref[cut(k), wide], ul_ref[cut(k), wide])
            a_ref[cut(i), wide] = a_ref[cut(i), wide] - product(a, b, TN)

        def carry(i, k=k):
            u = (uh_ref[cut(k), cut(i)], ul_ref[cut(k), cut(i)])
            r_ref[:, cut(i)] = r_ref[:, cut(i)] - product(halves(r_ref[:, cut(k)]), u, NN)

        if last:
            solve()
        else:
            if k + 2 < tiles:
                aside.append(functools.partial(trail, k + 1, k + 2))
            for i in range(k + 2, tiles):
                aside.append(functools.partial(trail, i, i))
            aside.append(solve)
            for i in range(k + 1, tiles):
                aside.append(functools.partial(carry, i))


def whiten(gram, s, scale):
    rows, rank = s.shape
    return pl.pallas_call(
        functools.partial(whiten_kernel, scale),
        out_shape=jax.ShapeDtypeStruct((rows, rank), bf16),
        scratch_shapes=[
            pltpu.VMEM((rank, rank), f32),
            pltpu.VMEM((rows, rank), f32),
            pltpu.VMEM((TILE, 2 * TILE), f32),
            pltpu.VMEM((TILE, TILE), f32),
            pltpu.VMEM((2 * PANEL * PANEL, TILE), f32),
            pltpu.VMEM((rank, rank), bf16),
            pltpu.VMEM((rank, rank), bf16),
        ],
        compiler_params=pltpu.CompilerParams(vmem_limit_bytes=32 * 1024 * 1024),
    )(gram, s)


PLANE = ("dir", "y", "core")


def scales_of(exponent_table):
    total = jnp.zeros(exponent_table.shape, jnp.float32)
    for exponent_value in range(-2, 3):
        total = total + jnp.where(
            exponent_table == exponent_value, jnp.float32(2.0**exponent_value), jnp.float32(0.0)
        )
    return total.astype(jnp.bfloat16)


def dequantize(values, exponent_table):
    height, breadth = values.shape
    edge_rows = height // exponent_table.shape[0]
    edge_cols = breadth // exponent_table.shape[1]
    scale_table = scales_of(exponent_table)
    tiled = values.reshape(exponent_table.shape[0], edge_rows, exponent_table.shape[1], edge_cols)
    tiled = tiled * scale_table[:, None, :, None]
    return tiled.reshape(height, breadth)


def exchange(pieces, count, axes):
    shape = pieces.shape
    paired = pieces.reshape(count, -1, 2, TILE)
    return lax.all_to_all(paired, axes, 0, 0).reshape(shape)


def sum_and_copy(pieces, count, copies):
    size = pieces.shape[0] // count
    chooser = jnp.asarray(np.tile(np.eye(size), (copies, count)), jnp.bfloat16)
    return jnp.dot(chooser, pieces, preferred_element_type=jnp.float32).astype(jnp.bfloat16)


def body(slab, exponents, sketch):
    scaled_values = dequantize(slab, exponents)
    partial_values = jnp.dot(scaled_values, sketch, preferred_element_type=jnp.float32)
    dirs, planes, depth = (lax.axis_size(axes) for axes in ("dir", PLANE, "z"))
    rank = sketch.shape[1]
    parts = partial_values.astype(jnp.bfloat16).reshape(dirs, -1, rank)
    parts = lax.all_to_all(parts, "dir", 0, 0)

    tiles = rank // TILE
    distinct = tiles * tiles // 2 * TILE + tiles // 2
    height = -(-distinct // (2 * planes)) * 2 * planes
    sketched, gram = local_gram(parts, height)
    gram = exchange(gram, planes, PLANE)
    gram = exchange(sum_and_copy(gram, planes, depth), depth, "z")
    gram = exchange(sum_and_copy(gram, depth, planes), planes, PLANE)
    texel_count = sketched.shape[0] * planes * depth
    return whiten(gram, sketched, math.sqrt(texel_count))


def solution(mesh):
    fine = Mesh(mesh.devices.reshape(4, 16, 4, 2), ("dir", "z", "y", "core"))
    tex = ("z", "y", "core")
    return jax.shard_map(
        body,
        mesh=fine,
        in_specs=(P(tex, "dir"), P(tex, "dir"), P("dir", None)),
        out_specs=P(tex + ("dir",), None),
        check_vma=False,
    )
```

time: 233 us -> 95.9 us (0.41)
  other arithmetic: 122 us -> 0.84 us
  local copies, waits for them, and re-layouts: 17.6 us -> 1.09 us
  blocking collectives: 63 us -> 77.6 us
  Pallas kernels: 0 us -> 13.8 us
  waiting for transfers between devices: 9.45 us -> 0 us
  matrix products: 11.4 us -> 2.28 us
  starting transfers between devices: 6.65 us -> 0 us
  between operations: 2.92 us -> 0.05 us
    another operation x17 -> x0, other arithmetic: 121 us -> none  [the longest x14 79.3 us: body(): lower_factor = jnp.linalg.cholesky(gram, symmetrize_input=False)]
    all_to_all x3 -> x4, blocking collectives: 63 us -> 77.6 us  [the longest x3 62.3 us: exchange(): return lax.all_to_all(paired, axes, 0, 0).reshape(shape)]
    another operation x16 -> x0, local copies, waits for them, and re-layouts: 13.8 us -> none
    pallas_call x0 -> x2, Pallas kernels: none -> 13.8 us  [the longest x1 13.4 us: whiten(): pl.pallas_call(functools.partial(whiten_kernel, scale), out_shape=jax.Sha...]
    all_to_all x1 -> x0, waiting for transfers between devices: 9.45 us -> none  [body(): lax.all_to_all(copies(mine, planes), PLANE, 0, 0).reshape(-1, TILE, TILE)]
    another operation x13 -> x0, matrix products: 9.32 us -> none  [the longest x7 5.74 us: right_solve(): lax.linalg.triangular_solve(lower_factor, matrix, left_side=False, lower=...]
    all_to_all x1 -> x0, starting transfers between devices: 6.65 us -> none  [body(): lax.all_to_all(copies(mine, planes), PLANE, 0, 0).reshape(-1, TILE, TILE)]
  transfers between devices with their start and end apart: 1 -> 0, of which waited for: 1 -> 0; matrix products, arithmetic and copies ran while one was open for 0% -> 0% of each run, Pallas kernels for 0% -> 0%
where the time goes in v3:
time: 95.9 us; the launch traced here: 95.7 us
  blocking collectives  77.6 us (81%)
  Pallas kernels  13.8 us (14%)
  matrix products  2.28 us (2%)
  local copies, waits for them, and re-layouts  1.09 us (1%)
    all_to_all x3, blocking collectives, exchange(): return lax.all_to_all(paired, axes, 0, 0).reshape(shape)  62.3 us
    all_to_all x1, blocking collectives, body(): parts = lax.all_to_all(parts, 'dir', 0, 0)  15.2 us
    pallas_call x1, Pallas kernels, whiten(): pl.pallas_call(functools.partial(whiten_kernel, scale), out_shape=jax.Sha...  13.4 us

profile of v3, /device:TPU:1, one launch (start us, length us, event | category | flops | bytes accessed | tf_op | source)
XLA Modules:
  0.0 95.7 jit_solution(9680205588364302103)
XLA Ops:
  0.0 0.0 copy-start
  0.0 0.0 copy-start.3
  0.0 0.8 add_convert_fusion
  0.8 0.3 mul.11
  1.2 0.0 copy-done
  1.2 0.7 copy-done.3
  1.9 1.2 %fusion.2 = bf16[1024,512]{1,0:T(8,128)(2,1)S(1)} fusion(bf16[1024,512]{1,0:T(8,128)(2,1)S(1)} %copy-done, bf16[1024,1024]{1,0:T(8,128)(2,1)S(1)} %copy-done.3, bf16[128,8,8,128]{3,2,1,0:T(8,128)(2,1)S(1)} %bitcast.25), kind=kOutput, calls=%fused_computation.4 | convolution fusion | flops 1075314688 | bytes 6291456 | tf_op jit(solution)/shard_map/dot_general | solution.py:279
  3.2 0.0 copy-start.2
  3.2 15.2 %all_to_all.20.parts_ref = bf16[4,256,512]{2,1,0:T(8,128)(2,1)S(1)} all-to-all(bf16[4,256,512]{2,1,0:T(8,128)(2,1)S(1)} %bitcast.28), channel_id=1, replica_groups=mesh['dir'=4,'z'=16,'y'=4,'core'=2] {'dir'}, dimensions={0} | all-to-all | bytes 2097152 | tf_op jit(solution)/shard_map/all_to_all | solution.py:283
  18.4 0.0 copy-start.1
  18.4 0.4 shard_map.55
  18.9 19.8 %all_to_all.21 = bf16[32,17,2,128]{3,2,1,0:T(2,128)(2,1)S(1)} all-to-all(bf16[32,17,2,128]{3,2,1,0:T(2,128)(2,1)S(1)} %bitcast.24), channel_id=1, replica_groups=mesh['dir'=4,'z'=16,'y'=4,'core'=2] {'dir','y','core'}, dimensions={0} | all-to-all | bytes 557056 | tf_op jit(solution)/shard_map/all_to_all | solution.py:268
  38.6 0.0 copy-done.2
  38.6 0.5 convolution_convert_fusion.1
  39.1 26.9 %all_to_all.22 = bf16[16,17,2,128]{3,2,1,0:T(2,128)(2,1)S(1)} all-to-all(bf16[16,17,2,128]{3,2,1,0:T(2,128)(2,1)S(1)} %bitcast.29), channel_id=1, replica_groups=mesh['dir'=4,'z'=16,'y'=4,'core'=2] {'z'}, dimensions={0} | all-to-all | bytes 278528 | tf_op jit(solution)/shard_map/all_to_all | solution.py:268
  66.0 0.0 copy-done.1
  66.0 0.5 convolution_convert_fusion
  66.5 15.7 %all_to_all.23 = bf16[32,17,2,128]{3,2,1,0:T(2,128)(2,1)S(1)} all-to-all(bf16[32,17,2,128]{3,2,1,0:T(2,128)(2,1)S(1)} %bitcast.27), channel_id=1, replica_groups=mesh['dir'=4,'z'=16,'y'=4,'core'=2] {'dir','y','core'}, dimensions={0} | all-to-all | bytes 557056 | tf_op jit(solution)/shard_map/all_to_all | solution.py:268
  82.3 13.4 %shard_map.56 = bf16[256,512]{1,0:T(8,128)(2,1)} custom-call(bf16[1088,128]{1,0:T(8,128)(2,1)S(1)} %bitcast.23, bf16[256,512]{1,0:T(8,128)(2,1)S(1)} %get-tuple-element.8.s_ref), custom_call_target="tpu_custom_call" | custom-call | tf_op jit(solution)/shard_map/pallas_call | solution.py:227
Async XLA Ops:
  0.0 1.2 %copy-start = (bf16[1024,512]{1,0:T(8,128)(2,1)S(1)}, bf16[1024,512]{1,0:T(8,128)(2,1)}, u32[]{:S(2)}) copy-start(bf16[1024,512]{1,0:T(8,128)(2,1)} %param.7) | copy-start | bytes 3145732
  0.0 1.9 %copy-start.3 = (bf16[1024,1024]{1,0:T(8,128)(2,1)S(1)}, bf16[1024,1024]{1,0:T(8,128)(2,1)}, u32[]{:S(2)}) copy-start(bf16[1024,1024]{1,0:T(8,128)(2,1)} %param.5) | copy-start | bytes 6291460
  3.2 35.4 %copy-start.2 = (bf16[544,1088]{1,0:T(8,128)(2,1)S(1)}, bf16[544,1088]{1,0:T(8,128)(2,1)}, u32[]{:S(2)}) copy-start(bf16[544,1088]{1,0:T(8,128)(2,1)} %constant.26.clone) | copy-start | bytes 3551236
  18.4 47.5 %copy-start.1 = (bf16[1088,544]{1,0:T(8,128)(2,1)S(1)}, bf16[1088,544]{1,0:T(8,128)(2,1)}, u32[]{:S(2)}) copy-start(bf16[1088,544]{1,0:T(8,128)(2,1)} %constant.27.clone) | copy-start | bytes 3551236

commit v4 on v3

--- a/solution.py
+++ b/solution.py
@@ -161,26 +161,28 @@
     tiles = rank // TILE
     row, col = places()
     eye = jnp.where(row == col, 1.0, 0.0)
-    at = tiles // 2
-    offset = tiles // 2 * TILE + tiles * (tiles - 1) // 2 * TILE
-    tail = gram_ref[offset : offset + 16, :].astype(f32)
-    for i in range(0, tiles, 2):
+    across = tiles // 2
+    offset = (across + tiles * (tiles - 1) // 2) * TILE
+
+    def unpack(i):
         pair = gram_ref[cut(i // 2), :].astype(f32)
         turned = jnp.transpose(pair)
-        first = jnp.where(col >= row, pair, turned)
+        tail = gram_ref[offset : offset + 16, :].astype(f32)
         second = jnp.where(col < row, pair, turned)
         second = jnp.where(row == col, tail[i // 2 : i // 2 + 1, :], second)
-        if i == 0:
-            f_ref[:, 0:TILE] = first
-        else:
-            a_ref[cut(i), cut(i)] = first
+        if i > 0:
+            a_ref[cut(i), cut(i)] = jnp.where(col >= row, pair, turned)
         a_ref[cut(i + 1), cut(i + 1)] = second
-    for i in range(tiles):
+
+    def widen(i):
+        start = across + i * (tiles - 1) - i * (i - 1) // 2
         for j in range(i + 1, tiles):
-            a_ref[cut(i), cut(j)] = gram_ref[cut(at), :].astype(f32)
-            at += 1
-    r_ref[...] = s_ref[...].astype(f32)
-    aside = []
+            a_ref[cut(i), cut(j)] = gram_ref[cut(start + j - i - 1), :].astype(f32)
+
+    pair = gram_ref[cut(0), :].astype(f32)
+    f_ref[:, 0:TILE] = jnp.where(col >= row, pair, jnp.transpose(pair))
+    aside = [functools.partial(unpack, i) for i in range(0, tiles, 2)]
+    aside += [functools.partial(widen, i) for i in range(tiles - 1)]
     for k in range(tiles):
         f_ref[:, TILE : 2 * TILE] = eye
         factor(f_ref, w_ref, t_ref, aside)
@@ -188,14 +190,24 @@
         aside = []
         last = k == tiles - 1
         if not last:
-            rest = slice((k + 1) * TILE, rank)
-            u = halves(product(w, halves(a_ref[cut(k), rest]), NN))
-            uh_ref[cut(k), rest], ul_ref[cut(k), rest] = u
-            near = (u[0][:, 0:TILE], u[1][:, 0:TILE])
+            row_k = halves(a_ref[cut(k), (k + 1) * TILE : rank])
+            near = halves(product(w, (row_k[0][:, 0:TILE], row_k[1][:, 0:TILE]), NN))
             f_ref[:, 0:TILE] = a_ref[cut(k + 1), cut(k + 1)] - product(near, near, TN)
+            uh_ref[cut(k), cut(k + 1)], ul_ref[cut(k), cut(k + 1)] = near
+
+        def spread(k=k, w=w):
+            wide = slice((k + 2) * TILE, rank)
+            uh_ref[cut(k), wide], ul_ref[cut(k), wide] = halves(
+                product(w, halves(a_ref[cut(k), wide]), NN)
+            )
 
         def solve(k=k, w=w, last=last):
-            q = product(halves(r_ref[:, cut(k)]), w, NT)
+            own = s_ref[:, cut(k)] if k == 0 else r_ref[:, cut(k)]
+            if k == 0:
+                q = lax.dot_general(own, w[0], (NT, ((), ())), preferred_element_type=f32)
+                q = q + lax.dot_general(own, w[1], (NT, ((), ())), preferred_element_type=f32)
+            else:
+                q = product(halves(own), w, NT)
             out_ref[:, cut(k)] = (q * scale).astype(out_ref.dtype)
             if not last:
                 r_ref[:, cut(k)] = q
@@ -208,12 +220,14 @@
 
         def carry(i, k=k):
             u = (uh_ref[cut(k), cut(i)], ul_ref[cut(k), cut(i)])
-            r_ref[:, cut(i)] = r_ref[:, cut(i)] - product(halves(r_ref[:, cut(k)]), u, NN)
+            own = s_ref[:, cut(i)].astype(f32) if k == 0 else r_ref[:, cut(i)]
+            r_ref[:, cut(i)] = own - product(halves(r_ref[:, cut(k)]), u, NN)
 
         if last:
             solve()
         else:
             if k + 2 < tiles:
+                aside.append(spread)
                 aside.append(functools.partial(trail, k + 1, k + 2))
             for i in range(k + 2, tiles):
                 aside.append(functools.partial(trail, i, i))
@@ -262,10 +276,11 @@
     return tiled.reshape(height, breadth)
 
 
-def exchange(pieces, count, axes):
+def exchange(pieces, count, axes, order=None):
     shape = pieces.shape
     paired = pieces.reshape(count, -1, 2, TILE)
-    return lax.all_to_all(paired, axes, 0, 0).reshape(shape)
+    groups = None if order is None else [order]
+    return lax.all_to_all(paired, axes, 0, 0, axis_index_groups=groups).reshape(shape)
 
 
 def sum_and_copy(pieces, count, copies):
@@ -287,7 +302,8 @@
     height = -(-distinct // (2 * planes)) * 2 * planes
     sketched, gram = local_gram(parts, height)
     gram = exchange(gram, planes, PLANE)
-    gram = exchange(sum_and_copy(gram, planes, depth), depth, "z")
+    order = [(z + depth // 2) % depth for z in range(depth)]
+    gram = exchange(sum_and_copy(gram, planes, depth), depth, "z", order)
     gram = exchange(sum_and_copy(gram, depth, planes), planes, PLANE)
     texel_count = sketched.shape[0] * planes * depth
     return whiten(gram, sketched, math.sqrt(texel_count))

time: 95.9 us -> 91.7 us (0.956)
  blocking collectives: 77.6 us -> 73.4 us
    all_to_all x3, blocking collectives: 62.3 us -> 58.2 us  [exchange(): lax.all_to_all(paired, axes, 0, 0, axis_index_groups=groups).reshape(shape)]
where the time goes in v4:
time: 91.7 us; the launch traced here: 91.4 us
  blocking collectives  73.4 us (80%)
  Pallas kernels  13.7 us (15%)
  matrix products  2.28 us (2%)
  local copies, waits for them, and re-layouts  1.09 us (1%)
    all_to_all x3, blocking collectives, exchange(): lax.all_to_all(paired, axes, 0, 0, axis_index_groups=groups).reshape(shape)  58.2 us
    all_to_all x1, blocking collectives, body(): parts = lax.all_to_all(parts, 'dir', 0, 0)  15.2 us
    pallas_call x1, Pallas kernels, whiten(): pl.pallas_call(functools.partial(whiten_kernel, scale), out_shape=jax.Sha...  13.3 us

profile of v4, /device:TPU:1, one launch (start us, length us, event | category | flops | bytes accessed | tf_op | source)
XLA Modules:
  0.0 91.4 jit_solution(6321157200302925482)
XLA Ops:
  0.0 0.0 copy-start
  0.0 0.0 copy-start.3
  0.0 0.8 add_convert_fusion
  0.8 0.3 mul.11
  1.2 0.0 copy-done
  1.2 0.7 copy-done.3
  1.9 1.2 %fusion.2 = bf16[1024,512]{1,0:T(8,128)(2,1)S(1)} fusion(bf16[1024,512]{1,0:T(8,128)(2,1)S(1)} %copy-done, bf16[1024,1024]{1,0:T(8,128)(2,1)S(1)} %copy-done.3, bf16[128,8,8,128]{3,2,1,0:T(8,128)(2,1)S(1)} %bitcast.25), kind=kOutput, calls=%fused_computation.4 | convolution fusion | flops 1075314688 | bytes 6291456 | tf_op jit(solution)/shard_map/dot_general | solution.py:294
  3.2 0.0 copy-start.2
  3.2 15.2 %all_to_all.20.parts_ref = bf16[4,256,512]{2,1,0:T(8,128)(2,1)S(1)} all-to-all(bf16[4,256,512]{2,1,0:T(8,128)(2,1)S(1)} %bitcast.28), channel_id=1, replica_groups=mesh['dir'=4,'z'=16,'y'=4,'core'=2] {'dir'}, dimensions={0} | all-to-all | bytes 2097152 | tf_op jit(solution)/shard_map/all_to_all | solution.py:298
  18.4 0.0 copy-start.1
  18.4 0.4 shard_map.55
  18.9 19.8 %all_to_all.21 = bf16[32,17,2,128]{3,2,1,0:T(2,128)(2,1)S(1)} all-to-all(bf16[32,17,2,128]{3,2,1,0:T(2,128)(2,1)S(1)} %bitcast.24), channel_id=1, replica_groups=mesh['dir'=4,'z'=16,'y'=4,'core'=2] {'dir','y','core'}, dimensions={0} | all-to-all | bytes 557056 | tf_op jit(solution)/shard_map/all_to_all | solution.py:283
  38.6 0.0 copy-done.2
  38.6 0.5 convolution_convert_fusion.1
  39.1 25.5 %all_to_all.22 = bf16[16,17,2,128]{3,2,1,0:T(2,128)(2,1)S(1)} all-to-all(bf16[16,17,2,128]{3,2,1,0:T(2,128)(2,1)S(1)} %bitcast.29), channel_id=1, replica_groups={{64,72,80,88,96,104,112,120,0,8,16,24,32,40,48,56},{65,73,81,89,97,105,..., dimensions={0} | all-to-all | bytes 278528 | tf_op jit(solution)/shard_map/all_to_all | solution.py:283
  64.6 0.0 copy-done.1
  64.6 0.5 convolution_convert_fusion
  65.2 12.9 %all_to_all.23 = bf16[32,17,2,128]{3,2,1,0:T(2,128)(2,1)S(1)} all-to-all(bf16[32,17,2,128]{3,2,1,0:T(2,128)(2,1)S(1)} %bitcast.27), channel_id=1, replica_groups=mesh['dir'=4,'z'=16,'y'=4,'core'=2] {'dir','y','core'}, dimensions={0} | all-to-all | bytes 557056 | tf_op jit(solution)/shard_map/all_to_all | solution.py:283
  78.1 13.3 %shard_map.56 = bf16[256,512]{1,0:T(8,128)(2,1)} custom-call(bf16[1088,128]{1,0:T(8,128)(2,1)S(1)} %bitcast.23, bf16[256,512]{1,0:T(8,128)(2,1)S(1)} %get-tuple-element.8.s_ref), custom_call_target="tpu_custom_call" | custom-call | tf_op jit(solution)/shard_map/pallas_call | solution.py:241
Async XLA Ops:
  0.0 1.2 %copy-start = (bf16[1024,512]{1,0:T(8,128)(2,1)S(1)}, bf16[1024,512]{1,0:T(8,128)(2,1)}, u32[]{:S(2)}) copy-start(bf16[1024,512]{1,0:T(8,128)(2,1)} %param.7) | copy-start | bytes 3145732
  0.0 1.9 %copy-start.3 = (bf16[1024,1024]{1,0:T(8,128)(2,1)S(1)}, bf16[1024,1024]{1,0:T(8,128)(2,1)}, u32[]{:S(2)}) copy-start(bf16[1024,1024]{1,0:T(8,128)(2,1)} %param.5) | copy-start | bytes 6291460
  3.2 35.4 %copy-start.2 = (bf16[544,1088]{1,0:T(8,128)(2,1)S(1)}, bf16[544,1088]{1,0:T(8,128)(2,1)}, u32[]{:S(2)}) copy-start(bf16[544,1088]{1,0:T(8,128)(2,1)} %constant.26.clone) | copy-start | bytes 3551236
  18.4 46.2 %copy-start.1 = (bf16[1088,544]{1,0:T(8,128)(2,1)S(1)}, bf16[1088,544]{1,0:T(8,128)(2,1)}, u32[]{:S(2)}) copy-start(bf16[1088,544]{1,0:T(8,128)(2,1)} %constant.27.clone) | copy-start | bytes 3551236

commit v5 on v4

--- a/solution.py
+++ b/solution.py
@@ -254,6 +254,7 @@
     )(gram, s)
 
 
+AXES = ("dir", "z", "y", "core")
 PLANE = ("dir", "y", "core")
 
 
@@ -276,11 +277,27 @@
     return tiled.reshape(height, breadth)
 
 
-def exchange(pieces, count, axes, order=None):
+def listed(axes, sizes, shifts):
+    names = tuple(sizes)
+    ids = np.arange(math.prod(sizes.values())).reshape(tuple(sizes.values()))
+    for name, shift in shifts.items():
+        ids = np.roll(ids, -shift, axis=names.index(name))
+    kept = [names.index(name) for name in names if name not in axes]
+    ids = ids.transpose(kept + [names.index(name) for name in axes])
+    width = math.prod(sizes[name] for name in axes)
+    return [[int(i) for i in group] for group in ids.reshape(-1, width)]
+
+
+def from_the_ends(group):
+    half = len(group) // 2
+    pairs = zip(group[half:], group[:half][::-1])
+    return group[:1] + [device for pair in pairs for device in pair][:-1]
+
+
+def exchange(pieces, groups):
     shape = pieces.shape
-    paired = pieces.reshape(count, -1, 2, TILE)
-    groups = None if order is None else [order]
-    return lax.all_to_all(paired, axes, 0, 0, axis_index_groups=groups).reshape(shape)
+    paired = pieces.reshape(len(groups[0]), -1, 2, TILE)
+    return lax.all_to_all(paired, AXES, 0, 0, axis_index_groups=groups).reshape(shape)
 
 
 def sum_and_copy(pieces, count, copies):
@@ -301,10 +318,13 @@
     distinct = tiles * tiles // 2 * TILE + tiles // 2
     height = -(-distinct // (2 * planes)) * 2 * planes
     sketched, gram = local_gram(parts, height)
-    gram = exchange(gram, planes, PLANE)
-    order = [(z + depth // 2) % depth for z in range(depth)]
-    gram = exchange(sum_and_copy(gram, planes, depth), depth, "z", order)
-    gram = exchange(sum_and_copy(gram, depth, planes), planes, PLANE)
+    sizes = {name: lax.axis_size(name) for name in AXES}
+    flat = listed(PLANE, sizes, {"dir": dirs // 2, "y": sizes["y"] // 2})
+    upright = listed(("z",), sizes, {"z": depth // 2})
+    upright = [from_the_ends(group) for group in upright]
+    gram = exchange(gram, flat)
+    gram = exchange(sum_and_copy(gram, planes, depth), upright)
+    gram = exchange(sum_and_copy(gram, depth, planes), flat)
     texel_count = sketched.shape[0] * planes * depth
     return whiten(gram, sketched, math.sqrt(texel_count))
 

time: 91.7 us -> 88.6 us (0.966)
  blocking collectives: 73.4 us -> 70.3 us
    all_to_all x3, blocking collectives: 58.2 us -> 55.1 us  [exchange(): lax.all_to_all(paired, AXES, 0, 0, axis_index_groups=groups).reshape(shape)]
where the time goes in v5:
time: 88.6 us; the launch traced here: 88.4 us
  blocking collectives  70.3 us (79%)
  Pallas kernels  13.7 us (15%)
  matrix products  2.28 us (3%)
  local copies, waits for them, and re-layouts  1.09 us (1%)
    all_to_all x3, blocking collectives, exchange(): lax.all_to_all(paired, AXES, 0, 0, axis_index_groups=groups).reshape(shape)  55.1 us
    all_to_all x1, blocking collectives, body(): parts = lax.all_to_all(parts, 'dir', 0, 0)  15.2 us
    pallas_call x1, Pallas kernels, whiten(): pl.pallas_call(functools.partial(whiten_kernel, scale), out_shape=jax.Sha...  13.3 us

profile of v5, /device:TPU:1, one launch (start us, length us, event | category | flops | bytes accessed | tf_op | source)
XLA Modules:
  0.0 88.4 jit_solution(4847783272787474170)
XLA Ops:
  0.0 0.0 copy-start
  0.0 0.0 copy-start.3
  0.0 0.8 add_convert_fusion
  0.8 0.3 mul.11
  1.2 0.0 copy-done
  1.2 0.7 copy-done.3
  1.9 1.2 %fusion.2 = bf16[1024,512]{1,0:T(8,128)(2,1)S(1)} fusion(bf16[1024,512]{1,0:T(8,128)(2,1)S(1)} %copy-done, bf16[1024,1024]{1,0:T(8,128)(2,1)S(1)} %copy-done.3, bf16[128,8,8,128]{3,2,1,0:T(8,128)(2,1)S(1)} %bitcast.25), kind=kOutput, calls=%fused_computation.4 | convolution fusion | flops 1075314688 | bytes 6291456 | tf_op jit(solution)/shard_map/dot_general | solution.py:311
  3.2 0.0 copy-start.2
  3.2 15.2 %all_to_all.20.parts_ref = bf16[4,256,512]{2,1,0:T(8,128)(2,1)S(1)} all-to-all(bf16[4,256,512]{2,1,0:T(8,128)(2,1)S(1)} %bitcast.28), channel_id=1, replica_groups=mesh['dir'=4,'z'=16,'y'=4,'core'=2] {'dir'}, dimensions={0} | all-to-all | bytes 2097152 | tf_op jit(solution)/shard_map/all_to_all | solution.py:315
  18.4 0.0 copy-start.1
  18.4 0.4 shard_map.55
  18.9 17.6 %all_to_all.21 = bf16[32,17,2,128]{3,2,1,0:T(2,128)(2,1)S(1)} all-to-all(bf16[32,17,2,128]{3,2,1,0:T(2,128)(2,1)S(1)} %bitcast.24), channel_id=1, replica_groups={{260,261,262,263,256,257,258,259,388,389,390,391,384,385,386,387,4,5,6,..., dimensions={0} | all-to-all | bytes 557056 | tf_op jit(solution)/shard_map/all_to_all | solution.py:300
  36.4 0.0 copy-done.2
  36.4 0.5 convolution_convert_fusion.1
  36.9 23.5 %all_to_all.22 = bf16[16,17,2,128]{3,2,1,0:T(2,128)(2,1)S(1)} all-to-all(bf16[16,17,2,128]{3,2,1,0:T(2,128)(2,1)S(1)} %bitcast.29), channel_id=1, replica_groups={{64,0,120,8,112,16,104,24,96,32,88,40,80,48,72,56},{65,1,121,9,113,17,1..., dimensions={0} | all-to-all | bytes 278528 | tf_op jit(solution)/shard_map/all_to_all | solution.py:300
  60.4 0.0 copy-done.1
  60.4 0.5 convolution_convert_fusion
  61.0 14.0 %all_to_all.23 = bf16[32,17,2,128]{3,2,1,0:T(2,128)(2,1)S(1)} all-to-all(bf16[32,17,2,128]{3,2,1,0:T(2,128)(2,1)S(1)} %bitcast.27), channel_id=1, replica_groups={{260,261,262,263,256,257,258,259,388,389,390,391,384,385,386,387,4,5,6,..., dimensions={0} | all-to-all | bytes 557056 | tf_op jit(solution)/shard_map/all_to_all | solution.py:300
  75.0 13.3 %shard_map.56 = bf16[256,512]{1,0:T(8,128)(2,1)} custom-call(bf16[1088,128]{1,0:T(8,128)(2,1)S(1)} %bitcast.23, bf16[256,512]{1,0:T(8,128)(2,1)S(1)} %get-tuple-element.8.s_ref), custom_call_target="tpu_custom_call" | custom-call | tf_op jit(solution)/shard_map/pallas_call | solution.py:241
Async XLA Ops:
  0.0 1.2 %copy-start = (bf16[1024,512]{1,0:T(8,128)(2,1)S(1)}, bf16[1024,512]{1,0:T(8,128)(2,1)}, u32[]{:S(2)}) copy-start(bf16[1024,512]{1,0:T(8,128)(2,1)} %param.7) | copy-start | bytes 3145732
  0.0 1.9 %copy-start.3 = (bf16[1024,1024]{1,0:T(8,128)(2,1)S(1)}, bf16[1024,1024]{1,0:T(8,128)(2,1)}, u32[]{:S(2)}) copy-start(bf16[1024,1024]{1,0:T(8,128)(2,1)} %param.5) | copy-start | bytes 6291460
  3.2 33.2 %copy-start.2 = (bf16[544,1088]{1,0:T(8,128)(2,1)S(1)}, bf16[544,1088]{1,0:T(8,128)(2,1)}, u32[]{:S(2)}) copy-start(bf16[544,1088]{1,0:T(8,128)(2,1)} %constant.26.clone) | copy-start | bytes 3551236
  18.4 42.0 %copy-start.1 = (bf16[1088,544]{1,0:T(8,128)(2,1)S(1)}, bf16[1088,544]{1,0:T(8,128)(2,1)}, u32[]{:S(2)}) copy-start(bf16[1088,544]{1,0:T(8,128)(2,1)} %constant.27.clone) | copy-start | bytes 3551236

commit v6 on v5

--- a/solution.py
+++ b/solution.py
@@ -255,7 +255,7 @@
 
 
 AXES = ("dir", "z", "y", "core")
-PLANE = ("dir", "y", "core")
+PLANE = ("core", "dir", "y")
 
 
 def scales_of(exponent_table):
@@ -312,15 +312,18 @@
     dirs, planes, depth = (lax.axis_size(axes) for axes in ("dir", PLANE, "z"))
     rank = sketch.shape[1]
     parts = partial_values.astype(jnp.bfloat16).reshape(dirs, -1, rank)
-    parts = lax.all_to_all(parts, "dir", 0, 0)
+    sizes = {name: lax.axis_size(name) for name in AXES}
+    middle = {name: sizes[name] // 2 for name in AXES[:-1]}
+    parts = jnp.roll(parts, -middle["dir"], axis=0)
+    row = listed(("dir",), sizes, {"dir": middle["dir"]})
+    parts = lax.all_to_all(parts, AXES, 0, 0, axis_index_groups=row)
 
     tiles = rank // TILE
     distinct = tiles * tiles // 2 * TILE + tiles // 2
     height = -(-distinct // (2 * planes)) * 2 * planes
     sketched, gram = local_gram(parts, height)
-    sizes = {name: lax.axis_size(name) for name in AXES}
-    flat = listed(PLANE, sizes, {"dir": dirs // 2, "y": sizes["y"] // 2})
-    upright = listed(("z",), sizes, {"z": depth // 2})
+    flat = listed(PLANE, sizes, {"dir": middle["dir"], "y": middle["y"]})
+    upright = listed(("z",), sizes, {"z": middle["z"]})
     upright = [from_the_ends(group) for group in upright]
     gram = exchange(gram, flat)
     gram = exchange(sum_and_copy(gram, planes, depth), upright)

time: 88.6 us -> 87.7 us (0.990)
  blocking collectives: 70.3 us -> 69.2 us
    all_to_all x1, blocking collectives: 15.2 us -> 13.5 us  [body(): parts = lax.all_to_all(parts, AXES, 0, 0, axis_index_groups=row)]
where the time goes in v6:
time: 87.7 us; the launch traced here: 87.4 us
  blocking collectives  69.2 us (79%)
  Pallas kernels  13.7 us (16%)
  matrix products  2.28 us (3%)
  local copies, waits for them, and re-layouts  1.16 us (1%)
  other arithmetic  0.94 us (1%)
    all_to_all x3, blocking collectives, exchange(): lax.all_to_all(paired, AXES, 0, 0, axis_index_groups=groups).reshape(shape)  55.7 us
    all_to_all x1, blocking collectives, body(): parts = lax.all_to_all(parts, AXES, 0, 0, axis_index_groups=row)  13.5 us
    pallas_call x1, Pallas kernels, whiten(): pl.pallas_call(functools.partial(whiten_kernel, scale), out_shape=jax.Sha...  13.3 us

profile of v6, /device:TPU:1, one launch (start us, length us, event | category | flops | bytes accessed | tf_op | source)
XLA Modules:
  0.0 87.4 jit_solution(7968682152922572523)
XLA Ops:
  0.0 0.0 copy-start
  0.0 0.0 copy-start.3
  0.0 0.8 add_convert_fusion
  0.8 0.3 mul.11
  1.2 0.0 copy-done
  1.2 0.7 copy-done.3
  1.9 1.2 %fusion.2 = bf16[1024,512]{1,0:T(8,128)(2,1)S(1)} fusion(bf16[1024,512]{1,0:T(8,128)(2,1)S(1)} %copy-done, bf16[1024,1024]{1,0:T(8,128)(2,1)S(1)} %copy-done.3, bf16[128,8,8,128]{3,2,1,0:T(8,128)(2,1)S(1)} %bitcast.26), kind=kOutput, calls=%fused_computation.4 | convolution fusion | flops 1075314688 | bytes 6291456 | tf_op jit(solution)/shard_map/dot_general | solution.py:311
  3.2 0.1 fusion.3
  3.3 0.1 pad_maximum_fusion
  3.4 0.0 copy-start.2
  3.4 13.5 %all_to_all.20.parts_ref = bf16[4,256,512]{2,1,0:T(8,128)(2,1)S(1)} all-to-all(bf16[4,256,512]{2,1,0:T(8,128)(2,1)S(1)} %pad_maximum_fusion), channel_id=1, replica_groups={{256,384,0,128},{257,385,1,129},{258,386,2,130},{259,387,3,131},{260,38..., dimensions={0} | all-to-all | bytes 2097152 | tf_op jit(solution)/shard_map/all_to_all | solution.py:319
  16.9 0.0 copy-start.1
  16.9 0.4 shard_map.55
  17.3 18.4 %all_to_all.21 = bf16[32,17,2,128]{3,2,1,0:T(2,128)(2,1)S(1)} all-to-all(bf16[32,17,2,128]{3,2,1,0:T(2,128)(2,1)S(1)} %bitcast.25), channel_id=1, replica_groups={{260,262,256,258,388,390,384,386,4,6,0,2,132,134,128,130,261,263,257,25..., dimensions={0} | all-to-all | bytes 557056 | tf_op jit(solution)/shard_map/all_to_all | solution.py:300
  35.6 0.0 copy-done.2
  35.6 0.5 convolution_convert_fusion.1
  36.1 23.3 %all_to_all.22 = bf16[16,17,2,128]{3,2,1,0:T(2,128)(2,1)S(1)} all-to-all(bf16[16,17,2,128]{3,2,1,0:T(2,128)(2,1)S(1)} %bitcast.31), channel_id=1, replica_groups={{64,0,120,8,112,16,104,24,96,32,88,40,80,48,72,56},{65,1,121,9,113,17,1..., dimensions={0} | all-to-all | bytes 278528 | tf_op jit(solution)/shard_map/all_to_all | solution.py:300
  59.5 0.0 copy-done.1
  59.5 0.5 convolution_convert_fusion
  60.0 14.1 %all_to_all.23 = bf16[32,17,2,128]{3,2,1,0:T(2,128)(2,1)S(1)} all-to-all(bf16[32,17,2,128]{3,2,1,0:T(2,128)(2,1)S(1)} %bitcast.30), channel_id=1, replica_groups={{260,262,256,258,388,390,384,386,4,6,0,2,132,134,128,130,261,263,257,25..., dimensions={0} | all-to-all | bytes 557056 | tf_op jit(solution)/shard_map/all_to_all | solution.py:300
  74.1 13.3 %shard_map.56 = bf16[256,512]{1,0:T(8,128)(2,1)} custom-call(bf16[1088,128]{1,0:T(8,128)(2,1)S(1)} %bitcast.24, bf16[256,512]{1,0:T(8,128)(2,1)S(1)} %get-tuple-element.8.s_ref), custom_call_target="tpu_custom_call" | custom-call | tf_op jit(solution)/shard_map/pallas_call | solution.py:241
Async XLA Ops:
  0.0 1.2 %copy-start = (bf16[1024,512]{1,0:T(8,128)(2,1)S(1)}, bf16[1024,512]{1,0:T(8,128)(2,1)}, u32[]{:S(2)}) copy-start(bf16[1024,512]{1,0:T(8,128)(2,1)} %param.7) | copy-start | bytes 3145732
  0.0 1.9 %copy-start.3 = (bf16[1024,1024]{1,0:T(8,128)(2,1)S(1)}, bf16[1024,1024]{1,0:T(8,128)(2,1)}, u32[]{:S(2)}) copy-start(bf16[1024,1024]{1,0:T(8,128)(2,1)} %param.5) | copy-start | bytes 6291460
  3.4 32.3 %copy-start.2 = (bf16[544,1088]{1,0:T(8,128)(2,1)S(1)}, bf16[544,1088]{1,0:T(8,128)(2,1)}, u32[]{:S(2)}) copy-start(bf16[544,1088]{1,0:T(8,128)(2,1)} %constant.26.clone) | copy-start | bytes 3551236
  16.9 42.6 %copy-start.1 = (bf16[1088,544]{1,0:T(8,128)(2,1)S(1)}, bf16[1088,544]{1,0:T(8,128)(2,1)}, u32[]{:S(2)}) copy-start(bf16[1088,544]{1,0:T(8,128)(2,1)} %constant.27.clone) | copy-start | bytes 3551236

commit v7 on v6

--- a/solution.py
+++ b/solution.py
@@ -28,10 +28,9 @@
 
 
 def product(a, b, dims):
-    def dot(x, y):
-        return lax.dot_general(x, y, (dims, ((), ())), preferred_element_type=f32)
-
-    return dot(a[0], b[0]) + (dot(a[0], b[1]) + dot(a[1], b[0]))
+    left = jnp.concatenate([a[0], a[0], a[1]], axis=dims[0][0])
+    right = jnp.concatenate([b[0], b[1], b[0]], axis=dims[1][0])
+    return lax.dot_general(left, right, (dims, ((), ())), preferred_element_type=f32)
 
 
 def places():
@@ -322,7 +321,7 @@
     distinct = tiles * tiles // 2 * TILE + tiles // 2
     height = -(-distinct // (2 * planes)) * 2 * planes
     sketched, gram = local_gram(parts, height)
-    flat = listed(PLANE, sizes, {"dir": middle["dir"], "y": middle["y"]})
+    flat = listed(PLANE, sizes, {"dir": middle["dir"], "y": middle["y"], "core": 1})
     upright = listed(("z",), sizes, {"z": middle["z"]})
     upright = [from_the_ends(group) for group in upright]
     gram = exchange(gram, flat)

time: 87.7 us -> 86.6 us (0.987)
  no operation moved by 1% of the time
where the time goes in v7:
time: 86.6 us; the launch traced here: 86.4 us
  blocking collectives  68.4 us (79%)
  Pallas kernels  13.5 us (16%)
  matrix products  2.28 us (3%)
  local copies, waits for them, and re-layouts  1.16 us (1%)
  other arithmetic  0.94 us (1%)
    all_to_all x3, blocking collectives, exchange(): lax.all_to_all(paired, AXES, 0, 0, axis_index_groups=groups).reshape(shape)  55 us
    all_to_all x1, blocking collectives, body(): parts = lax.all_to_all(parts, AXES, 0, 0, axis_index_groups=row)  13.5 us
    pallas_call x1, Pallas kernels, whiten(): pl.pallas_call(functools.partial(whiten_kernel, scale), out_shape=jax.Sha...  13.1 us

profile of v7, /device:TPU:1, one launch (start us, length us, event | category | flops | bytes accessed | tf_op | source)
XLA Modules:
  0.0 86.4 jit_solution(7452255453555484964)
XLA Ops:
  0.0 0.0 copy-start
  0.0 0.0 copy-start.3
  0.0 0.8 add_convert_fusion
  0.8 0.3 mul.11
  1.2 0.0 copy-done
  1.2 0.7 copy-done.3
  1.9 1.2 %fusion.2 = bf16[1024,512]{1,0:T(8,128)(2,1)S(1)} fusion(bf16[1024,512]{1,0:T(8,128)(2,1)S(1)} %copy-done, bf16[1024,1024]{1,0:T(8,128)(2,1)S(1)} %copy-done.3, bf16[128,8,8,128]{3,2,1,0:T(8,128)(2,1)S(1)} %bitcast.26), kind=kOutput, calls=%fused_computation.4 | convolution fusion | flops 1075314688 | bytes 6291456 | tf_op jit(solution)/shard_map/dot_general | solution.py:310
  3.2 0.1 fusion.3
  3.3 0.1 pad_maximum_fusion
  3.4 0.0 copy-start.2
  3.4 13.5 %all_to_all.20.parts_ref = bf16[4,256,512]{2,1,0:T(8,128)(2,1)S(1)} all-to-all(bf16[4,256,512]{2,1,0:T(8,128)(2,1)S(1)} %pad_maximum_fusion), channel_id=1, replica_groups={{256,384,0,128},{257,385,1,129},{258,386,2,130},{259,387,3,131},{260,38..., dimensions={0} | all-to-all | bytes 2097152 | tf_op jit(solution)/shard_map/all_to_all | solution.py:318
  16.9 0.0 copy-start.1
  16.9 0.4 shard_map.55
  17.3 18.0 %all_to_all.21 = bf16[32,17,2,128]{3,2,1,0:T(2,128)(2,1)S(1)} all-to-all(bf16[32,17,2,128]{3,2,1,0:T(2,128)(2,1)S(1)} %bitcast.25), channel_id=1, replica_groups={{261,263,257,259,389,391,385,387,5,7,1,3,133,135,129,131,260,262,256,25..., dimensions={0} | all-to-all | bytes 557056 | tf_op jit(solution)/shard_map/all_to_all | solution.py:299
  35.3 0.0 copy-done.2
  35.3 0.5 convolution_convert_fusion.1
  35.8 23.3 %all_to_all.22 = bf16[16,17,2,128]{3,2,1,0:T(2,128)(2,1)S(1)} all-to-all(bf16[16,17,2,128]{3,2,1,0:T(2,128)(2,1)S(1)} %bitcast.31), channel_id=1, replica_groups={{64,0,120,8,112,16,104,24,96,32,88,40,80,48,72,56},{65,1,121,9,113,17,1..., dimensions={0} | all-to-all | bytes 278528 | tf_op jit(solution)/shard_map/all_to_all | solution.py:299
  59.1 0.0 copy-done.1
  59.1 0.5 convolution_convert_fusion
  59.7 13.6 %all_to_all.23 = bf16[32,17,2,128]{3,2,1,0:T(2,128)(2,1)S(1)} all-to-all(bf16[32,17,2,128]{3,2,1,0:T(2,128)(2,1)S(1)} %bitcast.30), channel_id=1, replica_groups={{261,263,257,259,389,391,385,387,5,7,1,3,133,135,129,131,260,262,256,25..., dimensions={0} | all-to-all | bytes 557056 | tf_op jit(solution)/shard_map/all_to_all | solution.py:299
  73.3 13.1 %shard_map.56 = bf16[256,512]{1,0:T(8,128)(2,1)} custom-call(bf16[1088,128]{1,0:T(8,128)(2,1)S(1)} %bitcast.24, bf16[256,512]{1,0:T(8,128)(2,1)S(1)} %get-tuple-element.8.s_ref), custom_call_target="tpu_custom_call" | custom-call | tf_op jit(solution)/shard_map/pallas_call | solution.py:240
Async XLA Ops:
  0.0 1.2 %copy-start = (bf16[1024,512]{1,0:T(8,128)(2,1)S(1)}, bf16[1024,512]{1,0:T(8,128)(2,1)}, u32[]{:S(2)}) copy-start(bf16[1024,512]{1,0:T(8,128)(2,1)} %param.7) | copy-start | bytes 3145732
  0.0 1.9 %copy-start.3 = (bf16[1024,1024]{1,0:T(8,128)(2,1)S(1)}, bf16[1024,1024]{1,0:T(8,128)(2,1)}, u32[]{:S(2)}) copy-start(bf16[1024,1024]{1,0:T(8,128)(2,1)} %param.5) | copy-start | bytes 6291460
  3.4 31.9 %copy-start.2 = (bf16[544,1088]{1,0:T(8,128)(2,1)S(1)}, bf16[544,1088]{1,0:T(8,128)(2,1)}, u32[]{:S(2)}) copy-start(bf16[544,1088]{1,0:T(8,128)(2,1)} %constant.26.clone) | copy-start | bytes 3551236
  16.9 42.3 %copy-start.1 = (bf16[1088,544]{1,0:T(8,128)(2,1)S(1)}, bf16[1088,544]{1,0:T(8,128)(2,1)}, u32[]{:S(2)}) copy-start(bf16[1088,544]{1,0:T(8,128)(2,1)} %constant.27.clone) | copy-start | bytes 3551236

commit v8 on v7

--- a/solution.py
+++ b/solution.py
@@ -245,7 +245,7 @@
             pltpu.VMEM((rows, rank), f32),
             pltpu.VMEM((TILE, 2 * TILE), f32),
             pltpu.VMEM((TILE, TILE), f32),
-            pltpu.VMEM((2 * PANEL * PANEL, TILE), f32),
+            pltpu.VMEM((2 * PANEL * PANEL + PANEL, TILE), f32),
             pltpu.VMEM((rank, rank), bf16),
             pltpu.VMEM((rank, rank), bf16),
         ],

time: 86.6 us -> 86.6 us (level)
  no operation moved by 1% of the time
where the time goes in v8:
time: 86.6 us; the launch traced here: 86.4 us
  blocking collectives  68.4 us (79%)
  Pallas kernels  13.5 us (16%)
  matrix products  2.28 us (3%)
  local copies, waits for them, and re-layouts  1.16 us (1%)
  other arithmetic  0.94 us (1%)
    all_to_all x3, blocking collectives, exchange(): lax.all_to_all(paired, AXES, 0, 0, axis_index_groups=groups).reshape(shape)  55 us
    all_to_all x1, blocking collectives, body(): parts = lax.all_to_all(parts, AXES, 0, 0, axis_index_groups=row)  13.5 us
    pallas_call x1, Pallas kernels, whiten(): pl.pallas_call(functools.partial(whiten_kernel, scale), out_shape=jax.Sha...  13.1 us

profile of v8, /device:TPU:1, one launch (start us, length us, event | category | flops | bytes accessed | tf_op | source)
XLA Modules:
  0.0 86.4 jit_solution(17235122065739630051)
XLA Ops:
  0.0 0.0 copy-start
  0.0 0.0 copy-start.3
  0.0 0.8 add_convert_fusion
  0.8 0.3 mul.11
  1.2 0.0 copy-done
  1.2 0.7 copy-done.3
  1.9 1.2 %fusion.2 = bf16[1024,512]{1,0:T(8,128)(2,1)S(1)} fusion(bf16[1024,512]{1,0:T(8,128)(2,1)S(1)} %copy-done, bf16[1024,1024]{1,0:T(8,128)(2,1)S(1)} %copy-done.3, bf16[128,8,8,128]{3,2,1,0:T(8,128)(2,1)S(1)} %bitcast.26), kind=kOutput, calls=%fused_computation.4 | convolution fusion | flops 1075314688 | bytes 6291456 | tf_op jit(solution)/shard_map/dot_general | solution.py:310
  3.2 0.1 fusion.3
  3.3 0.1 pad_maximum_fusion
  3.4 0.0 copy-start.2
  3.4 13.5 %all_to_all.20.parts_ref = bf16[4,256,512]{2,1,0:T(8,128)(2,1)S(1)} all-to-all(bf16[4,256,512]{2,1,0:T(8,128)(2,1)S(1)} %pad_maximum_fusion), channel_id=1, replica_groups={{256,384,0,128},{257,385,1,129},{258,386,2,130},{259,387,3,131},{260,38..., dimensions={0} | all-to-all | bytes 2097152 | tf_op jit(solution)/shard_map/all_to_all | solution.py:318
  16.9 0.0 copy-start.1
  16.9 0.4 shard_map.55
  17.3 18.0 %all_to_all.21 = bf16[32,17,2,128]{3,2,1,0:T(2,128)(2,1)S(1)} all-to-all(bf16[32,17,2,128]{3,2,1,0:T(2,128)(2,1)S(1)} %bitcast.25), channel_id=1, replica_groups={{261,263,257,259,389,391,385,387,5,7,1,3,133,135,129,131,260,262,256,25..., dimensions={0} | all-to-all | bytes 557056 | tf_op jit(solution)/shard_map/all_to_all | solution.py:299
  35.3 0.0 copy-done.2
  35.3 0.5 convolution_convert_fusion.1
  35.8 23.3 %all_to_all.22 = bf16[16,17,2,128]{3,2,1,0:T(2,128)(2,1)S(1)} all-to-all(bf16[16,17,2,128]{3,2,1,0:T(2,128)(2,1)S(1)} %bitcast.31), channel_id=1, replica_groups={{64,0,120,8,112,16,104,24,96,32,88,40,80,48,72,56},{65,1,121,9,113,17,1..., dimensions={0} | all-to-all | bytes 278528 | tf_op jit(solution)/shard_map/all_to_all | solution.py:299
  59.1 0.0 copy-done.1
  59.1 0.5 convolution_convert_fusion
  59.7 13.6 %all_to_all.23 = bf16[32,17,2,128]{3,2,1,0:T(2,128)(2,1)S(1)} all-to-all(bf16[32,17,2,128]{3,2,1,0:T(2,128)(2,1)S(1)} %bitcast.30), channel_id=1, replica_groups={{261,263,257,259,389,391,385,387,5,7,1,3,133,135,129,131,260,262,256,25..., dimensions={0} | all-to-all | bytes 557056 | tf_op jit(solution)/shard_map/all_to_all | solution.py:299
  73.3 13.1 %shard_map.56 = bf16[256,512]{1,0:T(8,128)(2,1)} custom-call(bf16[1088,128]{1,0:T(8,128)(2,1)S(1)} %bitcast.24, bf16[256,512]{1,0:T(8,128)(2,1)S(1)} %get-tuple-element.8.s_ref), custom_call_target="tpu_custom_call" | custom-call | tf_op jit(solution)/shard_map/pallas_call | solution.py:240
Async XLA Ops:
  0.0 1.2 %copy-start = (bf16[1024,512]{1,0:T(8,128)(2,1)S(1)}, bf16[1024,512]{1,0:T(8,128)(2,1)}, u32[]{:S(2)}) copy-start(bf16[1024,512]{1,0:T(8,128)(2,1)} %param.7) | copy-start | bytes 3145732
  0.0 1.9 %copy-start.3 = (bf16[1024,1024]{1,0:T(8,128)(2,1)S(1)}, bf16[1024,1024]{1,0:T(8,128)(2,1)}, u32[]{:S(2)}) copy-start(bf16[1024,1024]{1,0:T(8,128)(2,1)} %param.5) | copy-start | bytes 6291460
  3.4 31.9 %copy-start.2 = (bf16[544,1088]{1,0:T(8,128)(2,1)S(1)}, bf16[544,1088]{1,0:T(8,128)(2,1)}, u32[]{:S(2)}) copy-start(bf16[544,1088]{1,0:T(8,128)(2,1)} %constant.26.clone) | copy-start | bytes 3551236
  16.9 42.3 %copy-start.1 = (bf16[1088,544]{1,0:T(8,128)(2,1)S(1)}, bf16[1088,544]{1,0:T(8,128)(2,1)}, u32[]{:S(2)}) copy-start(bf16[1088,544]{1,0:T(8,128)(2,1)} %constant.27.clone) | copy-start | bytes 3551236
